TPU v7x, 256 devices: a whole 4x4x8 slice. The times are simulated.
256 devices in a mesh: dp: 16 (over x, z_lo), expert: 16 (over z_hi, y, core).
Axes of the slice: x: 4, y: 4, z: 8 (z_hi: 2, z_lo: 4; z = z_hi * 4 + z_lo), core: 2. Of those that a mesh axis runs over, the one named last changes fastest.
Arguments:
- tokens: bfloat16 [8192, 4096], P('expert', 'dp'), may hold values from -6 to 6
- expert_ids: int32 [8192, 2], P('expert'), may hold values from 0 to 31, all different within a row; in each aligned block of 512 rows (0 to 511, 512 to 1023, ...) at most 64 rows name the same one
- gate_values: float32 [8192, 2], P('expert'), may hold values from 0.2 to 1
- w_in: bfloat16 [32, 4096, 1536], P('expert', 'dp'), may hold values from -0.09375 to 0.09375
- w_out: bfloat16 [32, 1536, 4096], P('expert', None, 'dp'), may hold values from -0.15625 to 0.15625
- grad_out: bfloat16 [8192, 4096], P('expert', 'dp'), may hold values from -3 to 3
Outputs:
- mixed: bfloat16 [8192, 4096], P('expert', 'dp')
- grad_tokens: bfloat16 [8192, 4096], P('expert', 'dp')
- grad_w_in: float32 [32, 4096, 1536], P('expert', 'dp')
- grad_w_out: float32 [32, 1536, 4096], P('expert', None, 'dp')
Inputs may be any that keep to these rules, and one draw needn't show every extreme that they name: `expert_ids`: each row names 2 different experts; among the 512 rows of one index of expert no expert is named by more than 64 rows, a bound that some block reaches.
All inputs are finite; a program needn't handle non-finite values.
Results may differ from a plain program's by a relative error of at most 0.03.
Values may be sent and summed in bfloat16 or wider, within the bound.
A program may use at most 128 MiB of HBM per device.

v0:
```python
import jax
import jax.numpy as jnp
from jax import lax
from jax.sharding import PartitionSpec as P

TOP = 2
EXP_DEV = 2


def gelu_value(pre):
    return jax.nn.gelu(pre, approximate=True)


def gelu_slope(pre):
    value, pullback = jax.vjp(gelu_value, pre)
    return pullback(jnp.ones_like(pre))[0]


def slot_index(expert_ids, num_experts, capacity):
    flat = expert_ids.reshape(-1)
    onehot = (flat[:, None] == jnp.arange(num_experts, dtype=jnp.int32)[None, :]).astype(jnp.int32)
    before = jnp.cumsum(onehot, axis=0) - onehot
    position = jnp.sum(before * onehot, axis=1)
    return flat * capacity + position


def sum_apart(partial_value):
    return lax.psum_scatter(
        partial_value.astype(jnp.bfloat16), "dp", scatter_dimension=0, tiled=True
    ).astype(jnp.float32)


def gather_apart(share):
    return lax.all_gather(share, "dp", axis=0, tiled=True)


def send_back(slot_rows):
    return lax.all_to_all(slot_rows, "expert", split_axis=0, concat_axis=0, tiled=True)


def body(tokens, expert_ids, gate_values, w_in, w_out, grad_out):
    groups = lax.axis_size("expert")
    tok_rows = tokens.shape[0]
    width = tokens.shape[1]
    hidden = w_in.shape[2]
    num_experts = EXP_DEV * groups
    capacity = 2 * tok_rows * TOP // num_experts
    total = num_experts * capacity
    slots = slot_index(expert_ids, num_experts, capacity)
    pair_rows = jnp.repeat(tokens, TOP, axis=0)
    scaled = (
        (gate_values[:, :, None] * grad_out[:, None, :].astype(jnp.float32))
        .astype(jnp.bfloat16)
        .reshape(tok_rows * TOP, width)
    )
    send_rows = (
        jnp.zeros((total, width), jnp.bfloat16)
        .at[slots]
        .set(pair_rows)
        .reshape(groups, EXP_DEV * capacity, width)
    )
    send_grads = (
        jnp.zeros((total, width), jnp.bfloat16)
        .at[slots]
        .set(scaled)
        .reshape(groups, EXP_DEV * capacity, width)
    )

    def inbound(rows):
        return rows.reshape(groups, EXP_DEV, capacity, width)

    got_rows = inbound(lax.all_to_all(send_rows, "expert", split_axis=0, concat_axis=0, tiled=True))
    pre_share = sum_apart(
        jnp.einsum("slcd,ldh->slch", got_rows, w_in, preferred_element_type=jnp.float32).reshape(
            -1, hidden
        )
    )
    act = gather_apart(gelu_value(pre_share).astype(jnp.bfloat16)).reshape(
        groups, EXP_DEV, capacity, hidden
    )
    result = jnp.einsum("slch,lhd->slcd", act, w_out, preferred_element_type=jnp.float32).astype(
        jnp.bfloat16
    )
    arrived = send_back(result.reshape(groups, EXP_DEV * capacity, width)).reshape(total, width)
    picked = arrived[slots].reshape(tok_rows, TOP, width).astype(jnp.float32)
    mixed = jnp.sum(gate_values[:, :, None] * picked, axis=1).astype(jnp.bfloat16)
    got_grads = inbound(
        lax.all_to_all(send_grads, "expert", split_axis=0, concat_axis=0, tiled=True)
    )
    slope_share = sum_apart(
        jnp.einsum("slcd,lhd->slch", got_grads, w_out, preferred_element_type=jnp.float32).reshape(
            -1, hidden
        )
    )
    delta = gather_apart((slope_share * gelu_slope(pre_share)).astype(jnp.bfloat16)).reshape(
        groups, EXP_DEV, capacity, hidden
    )
    grad_w_out = jnp.einsum("slch,slcd->lhd", act, got_grads, preferred_element_type=jnp.float32)
    grad_w_in = jnp.einsum("slcd,slch->ldh", got_rows, delta, preferred_element_type=jnp.float32)
    back = jnp.einsum("slch,ldh->slcd", delta, w_in, preferred_element_type=jnp.float32).astype(
        jnp.bfloat16
    )
    returned = send_back(back.reshape(groups, EXP_DEV * capacity, width)).reshape(total, width)
    gathered = returned[slots].reshape(tok_rows, TOP, width).astype(jnp.float32)
    grad_tokens = jnp.sum(gathered, axis=1).astype(jnp.bfloat16)
    return (mixed, grad_tokens, grad_w_in, grad_w_out)


def solution(mesh):
    return jax.shard_map(
        body,
        mesh=mesh,
        in_specs=(
            P("expert", "dp"),
            P("expert", None),
            P("expert", None),
            P("expert", "dp", None),
            P("expert", None, "dp"),
            P("expert", "dp"),
        ),
        out_specs=(
            P("expert", "dp"),
            P("expert", "dp"),
            P("expert", "dp", None),
            P("expert", None, "dp"),
        ),
        check_vma=False,
    )
```

profile of v0, /device:TPU:8, one launch (start us, length us, event | category | flops | bytes accessed | tf_op | source)
XLA Modules:
  0.0 745.5 jit_solution(10159270436512219492)
XLA Ops:
  7.2 0.0 copy-start
  7.2 0.0 reduce-scatter.5.cloned.1.call-start
  7.2 0.9 copy.13
  8.2 0.2 eq.29
  8.3 0.2 eq.25
  8.5 0.7 broadcast_multiply_fusion
  9.2 9.0 %reduce-window.6 = s32[32,8,128]{2,1,0:T(8,128)S(1)} reduce-window(s32[32,8,128]{2,1,0:T(8,128)S(1)} %fusion.48, s32[]{:T(128)} %constant.6.clone.1), window={size=1x1x128 pad=0_0x0_0x127_0}, to_apply=%region_0.0 | reduce-window | flops 4161536 | bytes 262148 | tf_op jit(solution)/shard_map/reduce-window
  18.2 0.1 slice.12
  18.3 0.1 copy.15
  18.5 0.1 copy.16
  18.6 0.1 broadcast_add_fusion
  18.7 0.1 copy.12
  18.8 0.2 mul.92
  19.0 0.8 copy.11
  19.9 0.2 mul.99
  20.0 2.2 mul.101
  22.2 1.9 mul.102
  24.2 6.5 scatter_custom_fusion.1
  30.7 30.8 %all_to_all.20 = bf16[16,128,256]{2,1,0:T(8,128)(2,1)S(1)} all-to-all(bf16[16,128,256]{2,1,0:T(8,128)(2,1)} %bitcast.77), channel_id=1, replica_groups=mesh['dp'=16,'expert'=16] {'expert'}, dimensions={0} | all-to-all | bytes 2097152 | tf_op jit(solution)/shard_map/all_to_all | solution.py:88
  61.5 0.0 copy-start.2
  61.5 0.0 copy-done
  61.5 1.8 convert_bitcast_fusion
  63.4 3.3 copy.23
  66.7 0.0 copy-done.2
  66.7 0.0 reduce-scatter.5.cloned.1.call-update
  66.8 0.0 reduce-scatter.3.cloned.1.call-start
  66.8 0.9 copy-done.6
  67.7 0.3 broadcast_in_dim.2
  68.0 0.2 reshape.137
  68.2 5.3 scatter_custom_fusion
  73.5 43.5 %all_to_all.21 = bf16[16,128,256]{2,1,0:T(8,128)(2,1)S(1)} all-to-all(bf16[16,128,256]{2,1,0:T(8,128)(2,1)S(1)} %bitcast.79), channel_id=1, replica_groups=mesh['dp'=16,'expert'=16] {'expert'}, dimensions={0} | all-to-all | bytes 2097152 | tf_op jit(solution)/shard_map/all_to_all | solution.py:72
  117.0 3.6 convert_bitcast_fusion.1
  120.5 3.3 copy.18
  123.9 0.0 copy-done.4
  123.9 0.0 reduce-scatter.3.cloned.1.call-update
  123.9 0.0 all-gather.3.cloned.1.call-start
  124.0 116.1 %reduce-scatter.5.cloned.1.call-done = bf16[128,1536]{1,0:T(8,128)(2,1)} async-done(((bf16[2048,1536]{1,0:T(8,128)(2,1)}), bf16[128,1536]{1,0:T(8,128)(2,1)}) %reduce-scatter.5.cloned.1.call-update) | async-done | bytes 393232 | tf_op jit(solution)/shard_map/reduce_scatter | solution.py:28
  240.1 144.1 %reduce-scatter.3.cloned.1.call-done = bf16[128,1536]{1,0:T(8,128)(2,1)} async-done(((bf16[2048,1536]{1,0:T(8,128)(2,1)}), bf16[128,1536]{1,0:T(8,128)(2,1)}) %reduce-scatter.3.cloned.1.call-update) | async-done | bytes 393232 | tf_op jit(solution)/shard_map/reduce_scatter | solution.py:28
  384.2 2.6 fusion.34
  386.8 0.0 all-gather.3.cloned.1.call-update
  386.8 0.0 all-gather.5.cloned.1.call-start
  386.8 0.5 all-gather.5.cloned.1.call-update
  387.4 140.9 %all-gather.3.cloned.1.call-done = bf16[2048,1536]{1,0:T(8,128)(2,1)} async-done(((bf16[128,1536]{1,0:T(8,128)(2,1)}), bf16[2048,1536]{1,0:T(8,128)(2,1)}) %all-gather.3.cloned.1.call-update) | async-done | bytes 6291472 | tf_op jit(solution)/shard_map/all_gather | solution.py:34
  528.3 4.6 fusion.23
  532.9 1.0 copy.20
  533.9 7.3 all-to-all-start.1
  541.2 152.5 %all-gather.5.cloned.1.call-done = bf16[2048,1536]{1,0:T(8,128)(2,1)} async-done(((bf16[128,1536]{1,0:T(8,128)(2,1)}), bf16[2048,1536]{1,0:T(8,128)(2,1)}) %all-gather.5.cloned.1.call-update) | async-done | bytes 6291472 | tf_op jit(solution)/shard_map/all_gather | solution.py:34
  693.8 5.1 fusion.18
  698.9 1.1 copy.25
  700.0 0.0 all-to-all-done.1
  700.0 7.3 all-to-all-start.3
  707.3 0.0 copy-done.3
  707.3 0.0 copy-start.5
  707.3 7.1 convolution_bitcast_fusion
  714.4 0.0 copy-done.5
  714.4 6.3 convolution_bitcast_fusion.1
  720.7 3.9 gather_fusion
  724.7 0.5 reshape.116
  725.2 3.6 multiply_reduce_fusion
  728.8 3.1 all-to-all-done.3
  731.9 4.8 gather_fusion.1
  736.7 0.2 reshape.115
  736.9 2.1 reduce_sum.35
  739.0 0.0 copy-done.1
  (10 shorter events, 0.1 us)
Async XLA Ops:
  7.2 54.4 %copy-start = (bf16[2,1536,256]{2,1,0:T(8,128)(2,1)S(1)}, bf16[2,1536,256]{2,1,0:T(8,128)(2,1)}, u32[]{:S(2)}) copy-start(bf16[2,1536,256]{2,1,0:T(8,128)(2,1)} %param.10) | copy-start | bytes 4718596
  7.2 232.9 %reduce-scatter.5.cloned.1.call-start = ((), (), s32[]{:S(2)}) async-start(), calls=%async_computation.8 | async-start | bytes 6684672 | tf_op jit(solution)/shard_map/reduce_scatter | solution.py:28
  61.5 5.2 copy-start.2
  66.7 1.0 copy-start.6
  66.8 317.4 %reduce-scatter.3.cloned.1.call-start = ((), (), s32[]{:S(2)}) async-start(), calls=%async_computation.6 | async-start | bytes 6684672 | tf_op jit(solution)/shard_map/reduce_scatter | solution.py:28
  117.0 6.9 copy-start.4
  123.9 404.4 %all-gather.3.cloned.1.call-start = ((), (), s32[]{:S(2)}) async-start(), calls=%async_computation.7 | async-start | bytes 6684672 | tf_op jit(solution)/shard_map/all_gather | solution.py:34
  386.8 307.0 %all-gather.5.cloned.1.call-start = ((), (), s32[]{:S(2)}) async-start(), calls=%async_computation.9 | async-start | bytes 6684672 | tf_op jit(solution)/shard_map/all_gather | solution.py:34
  533.9 166.1 %all-to-all-start.1 = ((bf16[16,128,256]{2,1,0:T(8,128)(2,1)}), bf16[16,128,256]{2,1,0:T(8,128)(2,1)S(1)}, u32[]{:S(2)}, u32[]{:S(2)}) async-start(bf16[16,128,256]{2,1,0:T(8,128)(2,1)} %bitcast.14), calls=%async_computation.2 | async-start | bytes 2097152 | tf_op jit(solution)/shard_map/all_to_all | solution.py:38
  693.8 13.6 %copy-start.3 = (bf16[16,128,256]{2,1,0:T(8,128)(2,1)S(1)}, bf16[16,128,256]{2,1,0:T(8,128)(2,1)}, u32[]{:S(2)}) copy-start(bf16[16,128,256]{2,1,0:T(8,128)(2,1)} %copy-done.2) | copy-start | bytes 3145732
  700.0 31.9 %all-to-all-start.3 = ((bf16[16,128,256]{2,1,0:T(8,128)(2,1)}), bf16[16,128,256]{2,1,0:T(8,128)(2,1)}, u32[]{:S(2)}, u32[]{:S(2)}) async-start(bf16[16,128,256]{2,1,0:T(8,128)(2,1)} %bitcast.78), calls=%async_computation.5 | async-start | bytes 2097152 | tf_op jit(solution)/shard_map/all_to_all | solution.py:38
  707.3 7.1 copy-start.5
  720.7 18.3 %copy-start.1 = (bf16[2,1536,256]{2,1,0:T(8,128)(2,1)S(1)}, bf16[2,1536,256]{2,1,0:T(8,128)(2,1)}, u32[]{:S(2)}) copy-start(bf16[2,1536,256]{2,1,0:T(8,128)(2,1)} %param.10) | copy-start | bytes 4718596
Sparse Core Ops, SparseCore 0:
  66.9 173.1 reduce-scatter.4
  242.7 141.4 reduce-scatter.2
  386.9 141.3 all-gather.2
  529.9 163.7 all-gather.4
where the time goes:
time: 751 us; the launch traced here: 746 us
  waiting for transfers between devices  557 us (74%)
  blocking collectives  74.3 us (10%)
  local copies, waits for them, and re-layouts  32 us (4%)
  matrix products  28.5 us (4%)
  other arithmetic  24.6 us (3%)
  starting transfers between devices  14.8 us (2%)
  between operations  14 us (2%)
    all_gather x2, waiting for transfers between devices, gather_apart(): return lax.all_gather(share, 'dp', axis=0, tiled=True)  293 us
    reduce_scatter x2, waiting for transfers between devices, sum_apart(): lax.psum_scatter(partial_value.astype(jnp.bfloat16), 'dp', scatter_dimens...  260 us
    all_to_all x1, blocking collectives, body(): lax.all_to_all(send_rows, 'expert', split_axis=0, concat_axis=0, tiled=True)  43.5 us
    all_to_all x1, blocking collectives, body(): lax.all_to_all(send_grads, 'expert', split_axis=0, concat_axis=0, tiled=T...  30.8 us
  transfers between devices with their start and end apart: 6, of which 5 were waited for; matrix products, arithmetic and copies ran while one was open for 6% of the time, Pallas kernels for 0%

commit v1 on v0

--- a/solution.py
+++ b/solution.py
@@ -18,9 +18,11 @@
 
 def slot_index(expert_ids, num_experts, capacity):
     flat = expert_ids.reshape(-1)
-    onehot = (flat[:, None] == jnp.arange(num_experts, dtype=jnp.int32)[None, :]).astype(jnp.int32)
-    before = jnp.cumsum(onehot, axis=0) - onehot
-    position = jnp.sum(before * onehot, axis=1)
+    onehot = flat[:, None] == jnp.arange(num_experts, dtype=jnp.int32)[None, :]
+    order = jnp.arange(flat.shape[0], dtype=jnp.int32)
+    earlier = (order[None, :] < order[:, None]).astype(jnp.bfloat16)
+    before = jnp.dot(earlier, onehot.astype(jnp.bfloat16), preferred_element_type=jnp.float32)
+    position = jnp.sum(jnp.where(onehot, before, 0.0), axis=1).astype(jnp.int32)
     return flat * capacity + position
 
 

time: 751 us -> 743 us (0.989)
  other arithmetic: 24.6 us -> 15.4 us
    another operation x3 -> x0, other arithmetic: 9.15 us -> none
where the time goes in v1:
time: 743 us; the launch traced here: 737 us
  waiting for transfers between devices  557 us (75%)
  blocking collectives  74.3 us (10%)
  local copies, waits for them, and re-layouts  33.5 us (5%)
  matrix products  28.8 us (4%)
  other arithmetic  15.4 us (2%)
  starting transfers between devices  14.8 us (2%)
  between operations  13.9 us (2%)
    all_gather x2, waiting for transfers between devices, gather_apart(): return lax.all_gather(share, 'dp', axis=0, tiled=True)  293 us
    reduce_scatter x2, waiting for transfers between devices, sum_apart(): lax.psum_scatter(partial_value.astype(jnp.bfloat16), 'dp', scatter_dimens...  260 us
    all_to_all x1, blocking collectives, body(): lax.all_to_all(send_rows, 'expert', split_axis=0, concat_axis=0, tiled=True)  43.5 us
    all_to_all x1, blocking collectives, body(): lax.all_to_all(send_grads, 'expert', split_axis=0, concat_axis=0, tiled=T...  30.8 us
  transfers between devices with their start and end apart: 6, of which 5 were waited for; matrix products, arithmetic and copies ran while one was open for 6% of the time, Pallas kernels for 0%

profile of v1, /device:TPU:8, one launch (start us, length us, event | category | flops | bytes accessed | tf_op | source)
XLA Modules:
  0.0 737.4 jit_solution(17013250403119654196)
XLA Ops:
  7.2 0.0 copy-start
  7.2 0.0 reduce-scatter.5.cloned.1.call-start
  7.2 0.9 copy.13
  8.2 0.7 broadcast_multiply_fusion
  8.9 0.2 eq.15
  9.0 0.5 fusion.31
  9.6 0.1 copy.12
  9.7 0.2 mul.89
  9.9 0.8 copy.11
  10.8 0.2 mul.95
  10.9 2.2 mul.97
  13.1 1.9 mul.98
  15.1 6.5 scatter_custom_fusion.1
  21.6 30.8 %all_to_all.20 = bf16[16,128,256]{2,1,0:T(8,128)(2,1)S(1)} all-to-all(bf16[16,128,256]{2,1,0:T(8,128)(2,1)} %bitcast.59), channel_id=1, replica_groups=mesh['dp'=16,'expert'=16] {'expert'}, dimensions={0} | all-to-all | bytes 2097152 | tf_op jit(solution)/shard_map/all_to_all | solution.py:90
  52.4 0.0 copy-start.1
  52.4 1.0 copy-done.1
  53.4 0.0 copy-done
  53.4 1.8 convert_bitcast_fusion
  55.3 3.3 copy.20
  58.6 0.0 copy-start.4
  58.6 0.0 reduce-scatter.5.cloned.1.call-update
  58.6 0.0 reduce-scatter.3.cloned.1.call-start
  58.7 0.9 copy-done.4
  59.5 0.3 broadcast_in_dim.7
  59.8 0.2 reshape.124
  60.0 5.3 scatter_custom_fusion
  65.3 43.5 %all_to_all.21 = bf16[16,128,256]{2,1,0:T(8,128)(2,1)S(1)} all-to-all(bf16[16,128,256]{2,1,0:T(8,128)(2,1)S(1)} %bitcast.62), channel_id=1, replica_groups=mesh['dp'=16,'expert'=16] {'expert'}, dimensions={0} | all-to-all | bytes 2097152 | tf_op jit(solution)/shard_map/all_to_all | solution.py:74
  108.8 0.0 copy-start.2
  108.8 1.0 copy-done.2
  109.8 3.2 convert_bitcast_fusion.1
  113.0 3.3 copy.15
  116.3 0.0 reduce-scatter.3.cloned.1.call-update
  116.4 0.0 all-gather.3.cloned.1.call-start
  116.4 115.6 %reduce-scatter.5.cloned.1.call-done = bf16[128,1536]{1,0:T(8,128)(2,1)} async-done(((bf16[2048,1536]{1,0:T(8,128)(2,1)}), bf16[128,1536]{1,0:T(8,128)(2,1)}) %reduce-scatter.5.cloned.1.call-update) | async-done | bytes 393232 | tf_op jit(solution)/shard_map/reduce_scatter | solution.py:30
  232.0 144.1 %reduce-scatter.3.cloned.1.call-done = bf16[128,1536]{1,0:T(8,128)(2,1)} async-done(((bf16[2048,1536]{1,0:T(8,128)(2,1)}), bf16[128,1536]{1,0:T(8,128)(2,1)}) %reduce-scatter.3.cloned.1.call-update) | async-done | bytes 393232 | tf_op jit(solution)/shard_map/reduce_scatter | solution.py:30
  376.1 2.6 fusion.37
  378.6 0.0 all-gather.3.cloned.1.call-update
  378.7 0.0 all-gather.5.cloned.1.call-start
  378.7 0.5 all-gather.5.cloned.1.call-update
  379.3 140.9 %all-gather.3.cloned.1.call-done = bf16[2048,1536]{1,0:T(8,128)(2,1)} async-done(((bf16[128,1536]{1,0:T(8,128)(2,1)}), bf16[2048,1536]{1,0:T(8,128)(2,1)}) %all-gather.3.cloned.1.call-update) | async-done | bytes 6291472 | tf_op jit(solution)/shard_map/all_gather | solution.py:36
  520.2 4.6 fusion.24
  524.8 1.0 copy.17
  525.8 7.3 all-to-all-start.1
  533.1 152.5 %all-gather.5.cloned.1.call-done = bf16[2048,1536]{1,0:T(8,128)(2,1)} async-done(((bf16[128,1536]{1,0:T(8,128)(2,1)}), bf16[2048,1536]{1,0:T(8,128)(2,1)}) %all-gather.5.cloned.1.call-update) | async-done | bytes 6291472 | tf_op jit(solution)/shard_map/all_gather | solution.py:36
  685.7 5.0 fusion.19
  690.7 1.1 copy.22
  691.8 0.0 all-to-all-done.1
  691.8 7.3 all-to-all-start.3
  699.2 0.0 copy-start.3
  699.2 7.3 convolution_bitcast_fusion
  706.5 0.0 copy-done.3
  706.5 6.3 convolution_bitcast_fusion.1
  712.8 3.9 gather_fusion
  716.7 0.5 reshape.103
  717.2 3.6 multiply_reduce_fusion
  720.8 2.9 all-to-all-done.3
  723.7 4.8 gather_fusion.1
  728.6 0.2 reshape.102
  728.8 2.1 reduce_sum.32
  (3 shorter events, 0.0 us)
Async XLA Ops:
  7.2 46.3 %copy-start = (bf16[2,1536,256]{2,1,0:T(8,128)(2,1)S(1)}, bf16[2,1536,256]{2,1,0:T(8,128)(2,1)}, u32[]{:S(2)}) copy-start(bf16[2,1536,256]{2,1,0:T(8,128)(2,1)} %param.10) | copy-start | bytes 4718596
  7.2 224.8 %reduce-scatter.5.cloned.1.call-start = ((), (), s32[]{:S(2)}) async-start(), calls=%async_computation.8 | async-start | bytes 6684672 | tf_op jit(solution)/shard_map/reduce_scatter | solution.py:30
  52.4 1.0 copy-start.1
  58.6 0.9 copy-start.4
  58.6 317.4 %reduce-scatter.3.cloned.1.call-start = ((), (), s32[]{:S(2)}) async-start(), calls=%async_computation.6 | async-start | bytes 6684672 | tf_op jit(solution)/shard_map/reduce_scatter | solution.py:30
  108.8 1.0 copy-start.2
  116.4 403.8 %all-gather.3.cloned.1.call-start = ((), (), s32[]{:S(2)}) async-start(), calls=%async_computation.7 | async-start | bytes 6684672 | tf_op jit(solution)/shard_map/all_gather | solution.py:36
  378.7 307.0 %all-gather.5.cloned.1.call-start = ((), (), s32[]{:S(2)}) async-start(), calls=%async_computation.9 | async-start | bytes 6684672 | tf_op jit(solution)/shard_map/all_gather | solution.py:36
  525.8 166.0 %all-to-all-start.1 = ((bf16[16,128,256]{2,1,0:T(8,128)(2,1)}), bf16[16,128,256]{2,1,0:T(8,128)(2,1)S(1)}, u32[]{:S(2)}, u32[]{:S(2)}) async-start(bf16[16,128,256]{2,1,0:T(8,128)(2,1)} %bitcast.61), calls=%async_computation.2 | async-start | bytes 2097152 | tf_op jit(solution)/shard_map/all_to_all | solution.py:40
  691.8 31.9 %all-to-all-start.3 = ((bf16[16,128,256]{2,1,0:T(8,128)(2,1)}), bf16[16,128,256]{2,1,0:T(8,128)(2,1)}, u32[]{:S(2)}, u32[]{:S(2)}) async-start(bf16[16,128,256]{2,1,0:T(8,128)(2,1)} %bitcast.60), calls=%async_computation.5 | async-start | bytes 2097152 | tf_op jit(solution)/shard_map/all_to_all | solution.py:40
  699.2 7.4 copy-start.3
Sparse Core Ops, SparseCore 0:
  58.7 173.2 reduce-scatter.4
  234.5 141.4 reduce-scatter.2
  378.8 141.3 all-gather.2
  521.8 163.7 all-gather.4

commit v2 on v1

v2 whole, which is shorter than its diff:
```python
import functools

import jax
import jax.numpy as jnp
from jax import lax
from jax.experimental import pallas as pl
from jax.experimental.pallas import tpu as pltpu
from jax.sharding import PartitionSpec as P

TOP = 2
EXP_DEV = 2
MESH = pl.DeviceIdType.MESH
GROUPS = (
    (0, 640, (0, 1, 2, 3)),
    (640, 640, (1, 0, 2, 3)),
    (1280, 128, (2, 3, 0, 1)),
    (1408, 128, (2, 3, 1, 0)),
)
STEPS = 4
TILE = 128


def gelu_value(pre):
    return jax.nn.gelu(pre, approximate=True)


def gelu_parts(pre):
    scale, cubic = 0.7978845608028654, 0.044715
    square = pre * pre
    tanh = jnp.tanh(scale * (pre + cubic * square * pre))
    half = 0.5 * (1.0 + tanh)
    slope = half + 0.5 * pre * (1.0 - tanh * tanh) * (scale * (1.0 + 3.0 * cubic * square))
    return pre * half, slope


def slot_index(expert_ids, num_experts, capacity):
    flat = expert_ids.reshape(-1)
    onehot = flat[:, None] == jnp.arange(num_experts, dtype=jnp.int32)[None, :]
    order = jnp.arange(flat.shape[0], dtype=jnp.int32)
    earlier = (order[None, :] < order[:, None]).astype(jnp.bfloat16)
    before = jnp.dot(earlier, onehot.astype(jnp.bfloat16), preferred_element_type=jnp.float32)
    position = jnp.sum(jnp.where(onehot, before, 0.0), axis=1).astype(jnp.int32)
    return flat * capacity + position


def partners_of(dp):
    x, z = dp // 4, dp % 4
    x0, x1, z0, z1 = x % 2, x // 2, z % 2, z // 2
    flip = lambda b: 1 - b
    at = lambda a1, a0, c1, c0: (a1 * 2 + a0) * 4 + c1 * 2 + c0
    return (
        (at(x1, flip(x0), z1, z0), (x0 + x1) % 2),
        (at(flip(x1), flip(x0), z1, z0), x1),
        (at(x1, x0, z1, flip(z0)), z0),
        (at(x1, x0, flip(z1), z0), z1),
    )


def hidden_kernel(rows_ref, grads_ref, w_in_ref, w_out_ref, act_ref, delta_ref, *scratch):
    count = len(GROUPS)
    work = (scratch[0:count], scratch[count : 2 * count])
    recv = (scratch[2 * count : 3 * count], scratch[3 * count : 4 * count])
    rs_send, rs_recv, ag_send, ag_recv = scratch[4 * count :]
    dp, ex = lax.axis_index("dp"), lax.axis_index("expert")
    partners = partners_of(dp)
    total = rows_ref.shape[0]
    per_expert = total // EXP_DEV
    outs = (act_ref, delta_ref)

    barrier = pltpu.get_barrier_semaphore()
    for other, _ in partners:
        pl.semaphore_signal(barrier, inc=1, device_id=(other, ex), device_id_type=MESH)

    def partial_products(tensor, g):
        first, columns, _ = GROUPS[g]
        tile = 256

        def body(i, carry):
            at = pl.ds(pl.multiple_of(i * tile, tile), tile)
            expert = i // (per_expert // tile)
            if tensor == 0:
                value = jnp.dot(
                    rows_ref[at, :],
                    w_in_ref[expert, :, first : first + columns],
                    preferred_element_type=jnp.float32,
                )
            else:
                value = lax.dot_general(
                    grads_ref[at, :],
                    w_out_ref[expert, first : first + columns, :],
                    (((1,), (1,)), ((), ())),
                    preferred_element_type=jnp.float32,
                )
            work[tensor][g][at, :] = value.astype(jnp.bfloat16)
            return carry

        lax.fori_loop(0, total // tile, body, 0)

    offsets = [[0] for _ in GROUPS]
    for g, (_, _, order) in enumerate(GROUPS):
        for k in range(STEPS):
            offsets[g].append(offsets[g][k] + partners[order[k]][1] * (total >> (k + 1)))

    def rs_copy(tensor, g, k):
        other, bit = partners[GROUPS[g][2][k]]
        size = total >> (k + 1)
        start = pl.multiple_of(offsets[g][k] + (1 - bit) * size, TILE)
        return pltpu.make_async_remote_copy(
            src_ref=work[tensor][g].at[pl.ds(start, size), :],
            dst_ref=recv[tensor][g].at[pl.ds(total - 2 * size, size), :],
            send_sem=rs_send.at[tensor, g, k],
            recv_sem=rs_recv.at[tensor, g, k],
            device_id=(other, ex),
            device_id_type=MESH,
        )

    def ag_copy(tensor, g, k):
        other, _ = partners[GROUPS[g][2][k]]
        first, columns, _ = GROUPS[g]
        size = total >> (k + 1)
        held = outs[tensor].at[
            pl.ds(pl.multiple_of(offsets[g][k + 1], TILE), size), pl.ds(first, columns)
        ]
        return pltpu.make_async_remote_copy(
            src_ref=held,
            dst_ref=held,
            send_sem=ag_send.at[tensor, g, k],
            recv_sem=ag_recv.at[tensor, g, k],
            device_id=(other, ex),
            device_id_type=MESH,
        )

    def add(tensor, g, k):
        size = total >> (k + 1)
        tile = 64

        def body(i, carry):
            at = pl.ds(pl.multiple_of(offsets[g][k + 1] + i * tile, tile), tile)
            came = pl.ds(pl.multiple_of(total - 2 * size + i * tile, tile), tile)
            mine = work[tensor][g][at, :].astype(jnp.float32)
            work[tensor][g][at, :] = (
                mine + recv[tensor][g][came, :].astype(jnp.float32)
            ).astype(jnp.bfloat16)
            return carry

        lax.fori_loop(0, size // tile, body, 0)

    def activate(g):
        first, columns, _ = GROUPS[g]
        k = STEPS - 1
        size = total >> STEPS
        tile = 32

        def body(i, carry):
            at = pl.ds(pl.multiple_of(offsets[g][STEPS] + i * tile, tile), tile)
            came = pl.ds(pl.multiple_of(total - 2 * size + i * tile, tile), tile)
            for c in range(0, columns, 128):
                here = slice(c, c + 128)
                pre = work[0][g][at, here].astype(jnp.float32) + recv[0][g][came, here].astype(jnp.float32)
                rise = work[1][g][at, here].astype(jnp.float32) + recv[1][g][came, here].astype(jnp.float32)
                value, slope = gelu_parts(pre)
                act_ref[at, first + c : first + c + 128] = value.astype(jnp.bfloat16)
                delta_ref[at, first + c : first + c + 128] = (rise * slope).astype(jnp.bfloat16)
            return carry

        lax.fori_loop(0, size // tile, body, 0)

    todo = [(tensor, g) for tensor in (0, 1) for g in (2, 3, 0, 1)]
    for n, (tensor, g) in enumerate(todo):
        partial_products(tensor, g)
        if n == 0:
            pl.semaphore_wait(barrier, len(partners))
        rs_copy(tensor, g, 0).start()
    for k in range(STEPS):
        for tensor, g in todo:
            rs_copy(tensor, g, k).wait_recv()
            if k < STEPS - 1:
                add(tensor, g, k)
                rs_copy(tensor, g, k + 1).start()
    for _, g in todo[: len(GROUPS)]:
        activate(g)
        for tensor in (0, 1):
            ag_copy(tensor, g, STEPS - 1).start()
    for k in reversed(range(STEPS)):
        for tensor, g in todo:
            ag_copy(tensor, g, k).wait_recv()
            if k:
                ag_copy(tensor, g, k - 1).start()
    for k in range(STEPS):
        for tensor, g in todo:
            rs_copy(tensor, g, k).wait_send()
            ag_copy(tensor, g, k).wait_send()


def hidden(rows, grads, w_in, w_out):
    total, units = rows.shape[0], w_in.shape[2]
    out = jax.ShapeDtypeStruct((total, units), jnp.bfloat16)
    pair = [pltpu.VMEM((total, c), jnp.bfloat16) for _, c, _ in GROUPS]
    came = [pltpu.VMEM((total - total // 16, c), jnp.bfloat16) for _, c, _ in GROUPS]
    return pl.pallas_call(
        hidden_kernel,
        out_shape=(out, out),
        in_specs=[pl.BlockSpec(memory_space=pltpu.VMEM)] * 4,
        out_specs=[pl.BlockSpec(memory_space=pltpu.VMEM)] * 2,
        scratch_shapes=pair * 2 + came * 2 + [pltpu.SemaphoreType.DMA((2, len(GROUPS), STEPS))] * 4,
        compiler_params=pltpu.CompilerParams(
            collective_id=0, has_side_effects=True, vmem_limit_bytes=52 * 2**20
        ),
        name="hidden",
    )(rows, grads, w_in, w_out)


def exchange(slot_rows):
    return lax.all_to_all(slot_rows, "expert", split_axis=0, concat_axis=0, tiled=True)


def body(tokens, expert_ids, gate_values, w_in, w_out, grad_out):
    groups = lax.axis_size("expert")
    tok_rows, width = tokens.shape
    num_experts = EXP_DEV * groups
    capacity = 2 * tok_rows * TOP // num_experts
    total = num_experts * capacity
    slots = slot_index(expert_ids, num_experts, capacity)
    pair_rows = jnp.repeat(tokens, TOP, axis=0)
    scaled = (
        (gate_values[:, :, None] * grad_out[:, None, :].astype(jnp.float32))
        .astype(jnp.bfloat16)
        .reshape(tok_rows * TOP, width)
    )

    def dispatch(rows):
        sent = jnp.zeros((total, width), jnp.bfloat16).at[slots].set(rows)
        got = exchange(sent.reshape(groups, EXP_DEV * capacity, width))
        return got.reshape(groups, EXP_DEV, capacity, width).transpose(1, 0, 2, 3).reshape(total, width)

    def send_back(rows):
        by_source = rows.reshape(EXP_DEV, groups, capacity, width).transpose(1, 0, 2, 3)
        back = exchange(by_source.reshape(groups, EXP_DEV * capacity, width)).reshape(total, width)
        return back[slots].reshape(tok_rows, TOP, width).astype(jnp.float32)

    rows, grads = dispatch(pair_rows), dispatch(scaled)
    act, delta = hidden(rows, grads, w_in, w_out)
    by_expert = lambda a: a.reshape(EXP_DEV, groups * capacity, -1)
    act, delta, rows, grads = by_expert(act), by_expert(delta), by_expert(rows), by_expert(grads)
    product = functools.partial(jnp.einsum, preferred_element_type=jnp.float32)
    result = product("lrh,lhd->lrd", act, w_out).astype(jnp.bfloat16)
    back = product("lrh,ldh->lrd", delta, w_in).astype(jnp.bfloat16)
    mixed = jnp.sum(gate_values[:, :, None] * send_back(result), axis=1).astype(jnp.bfloat16)
    grad_tokens = jnp.sum(send_back(back), axis=1).astype(jnp.bfloat16)
    grad_w_out = product("lrh,lrd->lhd", act, grads)
    grad_w_in = product("lrd,lrh->ldh", rows, delta)
    return (mixed, grad_tokens, grad_w_in, grad_w_out)


def solution(mesh):
    return jax.shard_map(
        body,
        mesh=mesh,
        in_specs=(
            P("expert", "dp"),
            P("expert", None),
            P("expert", None),
            P("expert", "dp", None),
            P("expert", None, "dp"),
            P("expert", "dp"),
        ),
        out_specs=(
            P("expert", "dp"),
            P("expert", "dp"),
            P("expert", "dp", None),
            P("expert", None, "dp"),
        ),
        check_vma=False,
    )
```

time: 743 us -> 424 us (0.57)
  waiting for transfers between devices: 557 us -> 38.1 us
  Pallas kernels: 0 us -> 277 us
  blocking collectives: 74.3 us -> 0 us
  starting transfers between devices: 14.8 us -> 45 us
  between operations: 13.9 us -> 0.79 us
  local copies, waits for them, and re-layouts: 33.5 us -> 24.7 us
    all_gather x2 -> x0, waiting for transfers between devices: 293 us -> none  [gather_apart(): return lax.all_gather(share, 'dp', axis=0, tiled=True)]
    pallas_call x0 -> x1, Pallas kernels: none -> 277 us  [hidden(): pl.pallas_call(hidden_kernel, out_shape=(out, out), in_specs=[pl.BlockSpe...]
    reduce_scatter x2 -> x0, waiting for transfers between devices: 260 us -> none  [sum_apart(): lax.psum_scatter(partial_value.astype(jnp.bfloat16), 'dp', scatter_dimens...]
    all_to_all x2 -> x0, blocking collectives: 74.3 us -> none  [the longest x1 43.5 us: body(): lax.all_to_all(send_rows, 'expert', split_axis=0, concat_axis=0, tiled=True)]
    all_to_all x2 -> x4, waiting for transfers between devices: 2.9 us -> 38.1 us  [exchange(): lax.all_to_all(slot_rows, 'expert', split_axis=0, concat_axis=0, tiled=True)]
    all_to_all x2 -> x4, starting transfers between devices: 14.6 us -> 45 us  [exchange(): lax.all_to_all(slot_rows, 'expert', split_axis=0, concat_axis=0, tiled=True)]
    convert_element_type x5 -> x1, local copies, waits for them, and re-layouts: 9.33 us -> 1.55 us  [send_back(): return back[slots].reshape(tok_rows, TOP, width).astype(jnp.float32)]
    dot_general x6 -> x4, matrix products: 28.3 us -> 23.1 us  [the longest x1 7.26 us: body(): grad_w_out = product('lrh,lrd->lhd', act, grads)]
  transfers between devices with their start and end apart: 6 -> 4, of which waited for: 5 -> 3; matrix products, arithmetic and copies ran while one was open for 6% -> 9% of each run, Pallas kernels for 0% -> 0%
where the time goes in v2:
time: 424 us; the launch traced here: 422 us
  Pallas kernels  277 us (65%)
  starting transfers between devices  45 us (11%)
  waiting for transfers between devices  38.1 us (9%)
  local copies, waits for them, and re-layouts  24.7 us (6%)
  matrix products  23.7 us (6%)
  other arithmetic  12.8 us (3%)
    pallas_call x1, Pallas kernels, hidden(): pl.pallas_call(hidden_kernel, out_shape=(out, out), in_specs=[pl.BlockSpe...  277 us
    all_to_all x4, starting transfers between devices, exchange(): lax.all_to_all(slot_rows, 'expert', split_axis=0, concat_axis=0, tiled=True)  45 us
    all_to_all x4, waiting for transfers between devices, exchange(): lax.all_to_all(slot_rows, 'expert', split_axis=0, concat_axis=0, tiled=True)  38.1 us
    gather x2, local copies, waits for them, and re-layouts, send_back(): return back[slots].reshape(tok_rows, TOP, width).astype(jnp.float32)  8.87 us
  transfers between devices with their start and end apart: 4, of which 3 were waited for; matrix products, arithmetic and copies ran while one was open for 9% of the time, Pallas kernels for 0%

profile of v2, /device:TPU:8, one launch (start us, length us, event | category | flops | bytes accessed | tf_op | source)
XLA Modules:
  0.0 421.6 jit_solution(7232913564714309772)
XLA Ops:
  0.6 0.8 copy.15
  1.5 0.7 broadcast_multiply_fusion
  2.2 0.2 eq.15
  2.3 0.5 fusion.2
  2.9 0.1 copy.14
  3.0 0.0 copy-start.1
  3.0 0.2 mul.45
  3.2 0.8 copy.13
  4.1 0.2 mul.46
  4.2 1.2 mul.48
  5.5 0.7 mul.49
  6.2 6.5 %scatter_custom_fusion.1 = bf16[2048,256]{1,0:T(8,128)(2,1)} fusion(s32[1024]{0:T(1024)S(1)} %bitcast.49, f32[1024,256]{1,0:T(8,128)S(1)} %mul.49, f32[1024]{0:T(1024)S(1)} %mul.46, bf16[]{:T(256)} %constant.1.clone.1), kind=kCustom, calls=%fused_computation.12 | custom fusion | flops 524288 | bytes 2101250 | tf_op jit(solution)/shard_map/scatter | solution.py:232
  12.7 11.6 %all-to-all-start.1 = ((bf16[16,128,256]{2,1,0:T(8,128)(2,1)}), bf16[16,128,256]{2,1,0:T(8,128)(2,1)S(1)}, u32[]{:S(2)}, u32[]{:S(2)}) async-start(bf16[16,128,256]{2,1,0:T(8,128)(2,1)} %bitcast.6), calls=%async_computation.1 | async-start | bytes 2097152 | tf_op jit(solution)/shard_map/all_to_all | solution.py:214
  24.2 0.0 copy-done.1
  24.2 0.3 broadcast_in_dim.7
  24.5 0.2 reshape.136
  24.7 6.0 %scatter_custom_fusion = bf16[2048,256]{1,0:T(8,128)(2,1)} fusion(s32[1024]{0:T(1024)S(1)} %bitcast.50, bf16[1024,256]{1,0:T(8,128)(2,1)S(1)} %reshape.136, bf16[]{:T(256)} %constant.1.clone.1), kind=kCustom, calls=%fused_computation.15 | custom fusion | bytes 1048578 | tf_op jit(solution)/shard_map/scatter | solution.py:232
  30.7 10.9 %all-to-all-done.1 = bf16[16,128,256]{2,1,0:T(8,128)(2,1)S(1)} async-done(((bf16[16,128,256]{2,1,0:T(8,128)(2,1)}), bf16[16,128,256]{2,1,0:T(8,128)(2,1)S(1)}, u32[]{:S(2)}, u32[]{:S(2)}) %all-to-all-start.1) | async-done | bytes 1048608 | tf_op jit(solution)/shard_map/all_to_all | solution.py:214
  41.6 14.8 %all-to-all-start = ((bf16[16,128,256]{2,1,0:T(8,128)(2,1)}), bf16[16,128,256]{2,1,0:T(8,128)(2,1)S(1)}, u32[]{:S(2)}, u32[]{:S(2)}) async-start(bf16[16,128,256]{2,1,0:T(8,128)(2,1)} %bitcast.2), calls=%async_computation | async-start | bytes 2097152 | tf_op jit(solution)/shard_map/all_to_all | solution.py:214
  56.4 1.0 copy.18
  57.4 15.0 %all-to-all-done = bf16[16,128,256]{2,1,0:T(8,128)(2,1)S(1)} async-done(((bf16[16,128,256]{2,1,0:T(8,128)(2,1)}), bf16[16,128,256]{2,1,0:T(8,128)(2,1)S(1)}, u32[]{:S(2)}, u32[]{:S(2)}) %all-to-all-start) | async-done | bytes 1048608 | tf_op jit(solution)/shard_map/all_to_all | solution.py:214
  72.4 0.0 copy-start
  72.4 0.1 copy.16
  72.5 276.6 %hidden.1 = (bf16[2048,1536]{1,0:T(8,128)(2,1)}, bf16[2048,1536]{1,0:T(8,128)(2,1)}) custom-call(bf16[2048,256]{1,0:T(8,128)(2,1)S(1)} %bitcast.34, bf16[2048,256]{1,0:T(8,128)(2,1)} %bitcast.40, bf16[2,256,1536]{2,1,0:T(8,128)(2,1)} %w_in_ref.1, bf16[2,1536,256]{2,1,0:T(8,128)(2,1)} %w_out_ref.1), custom_call_target="tpu_custom_call" | custom-call | tf_op jit(solution)/shard_map/hidden/pallas_call | solution.py:200
  349.1 0.0 copy-done
  349.1 4.6 %convolution_convert_fusion.1 = bf16[2,1024,256]{2,1,0:T(8,128)(2,1)S(1)} fusion(bf16[2,1024,1536]{2,1,0:T(8,128)(2,1)} %bitcast.42, bf16[2,1536,256]{2,1,0:T(8,128)(2,1)S(1)} %copy-done), kind=kOutput, calls=%fused_computation.7 | convolution fusion | flops 1611137024 | bytes 8912896 | tf_op jit(solution)/shard_map/lrh,lhd->lrd/dot_general | solution.py:246
  353.7 1.0 copy.19
  354.7 7.2 %all-to-all-start.2 = ((bf16[16,128,256]{2,1,0:T(8,128)(2,1)}), bf16[16,128,256]{2,1,0:T(8,128)(2,1)S(1)}, u32[]{:S(2)}, u32[]{:S(2)}) async-start(bf16[16,128,256]{2,1,0:T(8,128)(2,1)} %bitcast.13), calls=%async_computation.2 | async-start | bytes 2097152 | tf_op jit(solution)/shard_map/all_to_all | solution.py:214
  361.9 5.0 %convolution_convert_fusion = bf16[2,1024,256]{2,1,0:T(8,128)(2,1)S(1)} fusion(bf16[2,1024,1536]{2,1,0:T(8,128)(2,1)} %bitcast.38, bf16[2,256,1536]{2,1,0:T(8,128)(2,1)} %w_in_ref.1), kind=kOutput, calls=%fused_computation.6 | convolution fusion | flops 1611137024 | bytes 8912896 | tf_op jit(solution)/shard_map/lrh,ldh->lrd/dot_general | solution.py:247
  366.9 1.1 copy.20
  368.0 12.2 %all-to-all-done.2 = bf16[16,128,256]{2,1,0:T(8,128)(2,1)S(1)} async-done(((bf16[16,128,256]{2,1,0:T(8,128)(2,1)}), bf16[16,128,256]{2,1,0:T(8,128)(2,1)S(1)}, u32[]{:S(2)}, u32[]{:S(2)}) %all-to-all-start.2) | async-done | bytes 1048608 | tf_op jit(solution)/shard_map/all_to_all | solution.py:214
  380.3 11.5 %all-to-all-start.3 = ((bf16[16,128,256]{2,1,0:T(8,128)(2,1)}), bf16[16,128,256]{2,1,0:T(8,128)(2,1)S(1)}, u32[]{:S(2)}, u32[]{:S(2)}) async-start(bf16[16,128,256]{2,1,0:T(8,128)(2,1)} %bitcast.44), calls=%async_computation.3 | async-start | bytes 2097152 | tf_op jit(solution)/shard_map/all_to_all | solution.py:214
  391.8 7.3 %fusion.10 = f32[2,1536,256]{2,1,0:T(8,128)} fusion(bf16[2,1024,1536]{2,1,0:T(8,128)(2,1)} %bitcast.43, bf16[2,1024,256]{2,1,0:T(8,128)(2,1)} %bitcast.41), kind=kOutput, calls=%fused_computation.23 | convolution fusion | flops 1610612736 | bytes 10485760 | tf_op jit(solution)/shard_map/lrh,lrd->lhd/dot_general | solution.py:250
  399.1 6.3 %fusion.9 = f32[2,256,1536]{2,1,0:T(8,128)} fusion(bf16[2,1024,256]{2,1,0:T(8,128)(2,1)S(1)} %bitcast.35, bf16[2,1024,1536]{2,1,0:T(8,128)(2,1)} %bitcast.39), kind=kOutput, calls=%fused_computation.22 | convolution fusion | flops 1610612736 | bytes 10485760 | tf_op jit(solution)/shard_map/lrd,lrh->ldh/dot_general | solution.py:251
  405.3 4.9 %gather_fusion = bf16[1024,256]{1,0:T(8,128)(2,1)} fusion(bf16[2048,256]{1,0:T(8,128)(2,1)S(1)} %bitcast.36, s32[1024]{0:T(1024)S(1)} %broadcast_clamp_fusion), kind=kCustom, calls=%fused_computation | custom fusion | bytes 1052672 | tf_op jit(solution)/shard_map/gather | solution.py:239
  410.3 1.5 reshape.115
  411.8 3.6 multiply_reduce_fusion
  415.4 0.0 all-to-all-done.3
  415.4 3.9 gather_fusion.1
  419.4 0.2 reshape.114
  419.6 2.1 reduce_sum.32
  (3 shorter events, 0.0 us)
Async XLA Ops:
  3.0 21.2 %copy-start.1 = (bf16[512,256]{1,0:T(8,128)(2,1)S(1)}, bf16[512,256]{1,0:T(8,128)(2,1)}, u32[]{:S(2)}) copy-start(bf16[512,256]{1,0:T(8,128)(2,1)} %param.6) | copy-start | bytes 786436
  12.7 28.9 %all-to-all-start.1 = ((bf16[16,128,256]{2,1,0:T(8,128)(2,1)}), bf16[16,128,256]{2,1,0:T(8,128)(2,1)S(1)}, u32[]{:S(2)}, u32[]{:S(2)}) async-start(bf16[16,128,256]{2,1,0:T(8,128)(2,1)} %bitcast.6), calls=%async_computation.1 | async-start | bytes 2097152 | tf_op jit(solution)/shard_map/all_to_all | solution.py:214
  41.6 30.8 %all-to-all-start = ((bf16[16,128,256]{2,1,0:T(8,128)(2,1)}), bf16[16,128,256]{2,1,0:T(8,128)(2,1)S(1)}, u32[]{:S(2)}, u32[]{:S(2)}) async-start(bf16[16,128,256]{2,1,0:T(8,128)(2,1)} %bitcast.2), calls=%async_computation | async-start | bytes 2097152 | tf_op jit(solution)/shard_map/all_to_all | solution.py:214
  72.4 276.7 %copy-start = (bf16[2,1536,256]{2,1,0:T(8,128)(2,1)S(1)}, bf16[2,1536,256]{2,1,0:T(8,128)(2,1)}, u32[]{:S(2)}) copy-start(bf16[2,1536,256]{2,1,0:T(8,128)(2,1)} %w_out_ref.1) | copy-start | bytes 4718596
  354.7 25.6 %all-to-all-start.2 = ((bf16[16,128,256]{2,1,0:T(8,128)(2,1)}), bf16[16,128,256]{2,1,0:T(8,128)(2,1)S(1)}, u32[]{:S(2)}, u32[]{:S(2)}) async-start(bf16[16,128,256]{2,1,0:T(8,128)(2,1)} %bitcast.13), calls=%async_computation.2 | async-start | bytes 2097152 | tf_op jit(solution)/shard_map/all_to_all | solution.py:214
  380.3 35.2 %all-to-all-start.3 = ((bf16[16,128,256]{2,1,0:T(8,128)(2,1)}), bf16[16,128,256]{2,1,0:T(8,128)(2,1)S(1)}, u32[]{:S(2)}, u32[]{:S(2)}) async-start(bf16[16,128,256]{2,1,0:T(8,128)(2,1)} %bitcast.44), calls=%async_computation.3 | async-start | bytes 2097152 | tf_op jit(solution)/shard_map/all_to_all | solution.py:214

commit v3 on v2

v3 whole, which is shorter than its diff:
```python
import functools

import jax
import jax.numpy as jnp
from jax import lax
from jax.experimental import pallas as pl
from jax.experimental.pallas import tpu as pltpu
from jax.sharding import PartitionSpec as P

TOP = 2
EXP_DEV = 2
MESH = pl.DeviceIdType.MESH
STEPS = 4
MATES = 8
GROUPS = (
    (256, (2, 0, 1, 3)),
    (256, (2, 1, 0, 3)),
    (256, (1, 0, 2, 3)),
    (256, (0, 1, 2, 3)),
    (256, (0, 1, 2, 3)),
    (256, (1, 0, 2, 3)),
)
FIRST = tuple(sum(c for c, _ in GROUPS[:g]) for g in range(len(GROUPS)))
ORDER = (
    80, 88, 48, 56, 64, 72, 176, 32, 184, 40, 168, 89, 144, 8, 160, 81, 152, 0, 185, 49, 177, 57, 128, 65,
    136, 33, 104, 90, 145, 41, 96, 82, 153, 9, 161, 1, 129, 50, 186, 34, 91, 178, 83, 66, 187, 137, 58, 146,
    51, 73, 105, 16, 179, 97, 10, 130, 35, 42, 162, 154, 24, 147, 59, 131, 39, 106, 138, 155, 43, 169, 2, 74,
    135, 38, 11, 139, 47, 120, 107, 63, 98, 25, 112, 17, 143, 3, 170, 46, 134, 37, 159, 62, 67, 99, 55, 121,
    26, 113, 163, 75, 142, 45, 18, 158, 61, 133, 36, 151, 54, 87, 171, 95, 183, 7, 122, 86, 150, 157, 114, 60,
    141, 44, 53, 191, 15, 103, 6, 19, 182, 94, 111, 27, 115, 23, 102, 85, 132, 5, 149, 14, 123, 31, 119, 71,
    190, 22, 110, 93, 127, 79, 167, 140, 13, 181, 101, 84, 175, 118, 30, 109, 156, 70, 189, 21, 92, 126, 29,
    78, 166, 52, 174, 4, 117, 69, 180, 125, 28, 20, 188, 77, 165, 148, 12, 100, 124, 173, 76, 68, 116, 108,
    172, 164,
)


def decoded(number):
    rest, k = divmod(number, STEPS)
    rest, gather = divmod(rest, 2)
    rest, g = divmod(rest, len(GROUPS))
    wait, tensor = divmod(rest, 2)
    return wait, tensor, g, gather, k


def gelu_parts(pre):
    scale, cubic = 0.7978845608028654, 0.044715
    square = pre * pre
    tanh = jnp.tanh(scale * (pre + cubic * square * pre))
    half = 0.5 * (1.0 + tanh)
    slope = half + 0.5 * pre * (1.0 - tanh * tanh) * (scale * (1.0 + 3.0 * cubic * square))
    return pre * half, slope


def slot_index(expert_ids, num_experts, capacity):
    flat = expert_ids.reshape(-1)
    onehot = flat[:, None] == jnp.arange(num_experts, dtype=jnp.int32)[None, :]
    order = jnp.arange(flat.shape[0], dtype=jnp.int32)
    earlier = (order[None, :] < order[:, None]).astype(jnp.bfloat16)
    before = jnp.dot(earlier, onehot.astype(jnp.bfloat16), preferred_element_type=jnp.float32)
    position = jnp.sum(jnp.where(onehot, before, 0.0), axis=1).astype(jnp.int32)
    return flat * capacity + position


def partners_of(dp):
    x, z = dp // 4, dp % 4
    x0, x1, z0, z1 = x % 2, x // 2, z % 2, z // 2

    def at(a1, a0, c1, c0):
        return (a1 * 2 + a0) * 4 + c1 * 2 + c0

    return (
        (at(x1, 1 - x0, z1, z0), (x0 + x1) % 2),
        (at(1 - x1, 1 - x0, z1, z0), x1),
        (at(x1, x0, z1, 1 - z0), z0),
        (at(x1, x0, 1 - z1, z0), z1),
    )


def layer_kernel(
    tokens_ref, grad_out_ref, info_ref, w_in_ref, w_out_ref, mixed_ref, grad_tokens_ref, gw_in_ref, gw_out_ref, *scratch
):
    count = len(GROUPS)
    work = (scratch[0:count], scratch[count : 2 * count])
    recv = (scratch[2 * count : 3 * count], scratch[3 * count : 4 * count])
    (
        act_ref, delta_ref, rows_ref, grads_ref, info_other, tokens_other, grad_out_other, hot, gate,
        sent, ret, half_sent, half_came,
        rs_send, rs_recv, ag_send, ag_recv, y_send, y_recv, b_send, b_recv, h_send, h_recv,
    ) = scratch[4 * count :]
    dp, ex = lax.axis_index("dp"), lax.axis_index("expert")
    zh, mate = ex // MATES, ex % MATES
    across = (1 - zh) * MATES + mate
    partners = partners_of(dp)
    tok_rows, width = tokens_ref.shape
    per_expert = rows_ref.shape[1]
    total = EXP_DEV * per_expert
    units = act_ref.shape[1]
    cap = per_expert // (2 * MATES)
    outs = (act_ref, delta_ref)
    routed = (rows_ref, grads_ref)

    barrier = pltpu.get_barrier_semaphore()
    for other, _ in partners:
        pl.semaphore_signal(barrier, inc=1, device_id=(other, ex), device_id_type=MESH)
    pl.semaphore_signal(barrier, inc=1, device_id=(dp, across), device_id_type=MESH)
    for j in range(1, MATES):
        near = zh * MATES + (mate + j) % MATES
        pl.semaphore_signal(barrier, inc=1, device_id=(dp, near), device_id_type=MESH)

    def build_map(b):
        source = info_ref if b == 0 else info_other
        tile = 128

        def body(i, carry):
            at = pl.ds(pl.multiple_of(i * tile, tile), tile)
            slot = (
                lax.broadcasted_iota(jnp.int32, (tile, tok_rows), 0) + (zh * per_expert + i * tile)
            ).astype(jnp.float32)
            first, second = source[0:1, :] == slot, source[1:2, :] == slot
            hot[b, at, :] = jnp.where(first, 1.0, jnp.where(second, 1.0, 0.0)).astype(jnp.bfloat16)
            weight = jnp.where(first, source[2:3, :], jnp.where(second, source[3:4, :], 0.0))
            gate[b, at, :] = jnp.broadcast_to(jnp.sum(weight, axis=1, keepdims=True), (tile, 128))
            return carry

        lax.fori_loop(0, per_expert // tile, body, 0)

    def here(b):
        return zh if b == 0 else 1 - zh

    def piece(owner, b):
        return pl.ds(pl.multiple_of((owner * 2 + here(b)) * cap, cap), cap)

    def route_copy(tensor, b, j):
        to = (mate + j) % MATES
        return pltpu.make_async_remote_copy(
            src_ref=sent.at[tensor, :, piece(to, b), :],
            dst_ref=routed[tensor].at[:, piece(mate, b), :],
            send_sem=y_send.at[tensor, b, j],
            recv_sem=y_recv.at[tensor, b, j],
            device_id=(dp, zh * MATES + to),
            device_id_type=MESH,
        )

    def route_wait(tensor, b, j):
        return route_copy(tensor, b, j).wait_recv()

    def dispatch(tensor, b):
        block = ((tokens_ref, grad_out_ref), (tokens_other, grad_out_other))[b][tensor]
        near = 4

        def body(i, carry):
            at = pl.ds(pl.multiple_of(i * near * 2 * cap, near * 2 * cap), near * 2 * cap)
            picked = jnp.dot(hot[b, at, :], block[...], preferred_element_type=jnp.float32)
            if tensor == 1:
                level = gate[b, at, :]
                picked = picked * jnp.concatenate([level] * (width // 128), axis=1)
            picked = picked.astype(jnp.bfloat16)
            for n in range(near):
                for e in range(EXP_DEV):
                    start = (n * EXP_DEV + e) * cap
                    sent[tensor, e, piece(i * near + n, b), :] = picked[start : start + cap, :]
            return carry

        lax.fori_loop(0, MATES // near, body, 0)

        def go(j, carry):
            route_copy(tensor, b, j).start()
            return carry

        lax.fori_loop(1, MATES, go, 0)
        routed[tensor][:, piece(mate, b), :] = sent[tensor, :, piece(mate, b), :]

    def arrived(tensor, b):
        def body(j, carry):
            route_wait(tensor, b, j)
            return carry

        lax.fori_loop(1, MATES, body, 0)

    def across_copy(n, source, target):
        return pltpu.make_async_remote_copy(
            src_ref=source,
            dst_ref=target,
            send_sem=h_send.at[n],
            recv_sem=h_recv.at[n],
            device_id=(dp, across),
            device_id_type=MESH,
        )

    def partial_products(tensor, g):
        columns, _ = GROUPS[g]
        first = FIRST[g]
        tile = 512

        def body(i, carry):
            expert = i // (per_expert // tile)
            inner = pl.ds(pl.multiple_of((i % (per_expert // tile)) * tile, tile), tile)
            if tensor == 0:
                value = jnp.dot(
                    rows_ref[expert, inner, :],
                    w_in_ref[expert, :, first : first + columns],
                    preferred_element_type=jnp.float32,
                )
            else:
                value = lax.dot_general(
                    grads_ref[expert, inner, :],
                    w_out_ref[expert, first : first + columns, :],
                    (((1,), (1,)), ((), ())),
                    preferred_element_type=jnp.float32,
                )
            work[tensor][g][pl.ds(pl.multiple_of(i * tile, tile), tile), :] = value.astype(jnp.bfloat16)
            return carry

        lax.fori_loop(0, total // tile, body, 0)

    offsets = [[0] for _ in GROUPS]
    for g, (_, order) in enumerate(GROUPS):
        for k in range(STEPS):
            offsets[g].append(offsets[g][k] + partners[order[k]][1] * (total >> (k + 1)))

    def rs_copy(tensor, g, k):
        other, bit = partners[GROUPS[g][1][k]]
        size = total >> (k + 1)
        start = pl.multiple_of(offsets[g][k] + (1 - bit) * size, 128)
        return pltpu.make_async_remote_copy(
            src_ref=work[tensor][g].at[pl.ds(start, size), :],
            dst_ref=recv[tensor][g].at[pl.ds(total - 2 * size, size), :],
            send_sem=rs_send.at[tensor, g, k],
            recv_sem=rs_recv.at[tensor, g, k],
            device_id=(other, ex),
            device_id_type=MESH,
        )

    def ag_copy(tensor, g, k):
        other, _ = partners[GROUPS[g][1][k]]
        size = total >> (k + 1)
        held = outs[tensor].at[
            pl.ds(pl.multiple_of(offsets[g][k + 1], 128), size), pl.ds(FIRST[g], GROUPS[g][0])
        ]
        return pltpu.make_async_remote_copy(
            src_ref=held,
            dst_ref=held,
            send_sem=ag_send.at[tensor, g, k],
            recv_sem=ag_recv.at[tensor, g, k],
            device_id=(other, ex),
            device_id_type=MESH,
        )

    def add(tensor, g, k):
        size = total >> (k + 1)
        tile = 128

        def body(i, carry):
            at = pl.ds(pl.multiple_of(offsets[g][k + 1] + i * tile, tile), tile)
            came = pl.ds(pl.multiple_of(total - 2 * size + i * tile, tile), tile)
            mine = work[tensor][g][at, :].astype(jnp.float32)
            work[tensor][g][at, :] = (
                mine + recv[tensor][g][came, :].astype(jnp.float32)
            ).astype(jnp.bfloat16)
            return carry

        lax.fori_loop(0, size // tile, body, 0)

    def activate(g):
        columns, _ = GROUPS[g]
        size = total >> STEPS
        tile = 32

        def body(i, carry):
            at = pl.ds(pl.multiple_of(offsets[g][STEPS] + i * tile, tile), tile)
            came = pl.ds(pl.multiple_of(total - 2 * size + i * tile, tile), tile)
            for c in range(0, columns, 128):
                part = slice(c, c + 128)
                there = slice(FIRST[g] + c, FIRST[g] + c + 128)
                pre = work[0][g][at, part].astype(jnp.float32) + recv[0][g][came, part].astype(jnp.float32)
                rise = work[1][g][at, part].astype(jnp.float32) + recv[1][g][came, part].astype(jnp.float32)
                value, slope = gelu_parts(pre)
                act_ref[at, there] = value.astype(jnp.bfloat16)
                delta_ref[at, there] = (rise * slope).astype(jnp.bfloat16)
            return carry

        lax.fori_loop(0, size // tile, body, 0)

    def back_copy(tensor, b, j):
        to = (mate + j) % MATES
        return pltpu.make_async_remote_copy(
            src_ref=sent.at[tensor, :, piece(to, b), :],
            dst_ref=ret.at[tensor, b, mate],
            send_sem=b_send.at[tensor, b, j],
            recv_sem=b_recv.at[tensor, b, j],
            device_id=(dp, zh * MATES + to),
            device_id_type=MESH,
        )

    def results(tensor):
        tile = 512

        def body(i, carry):
            expert = i // (per_expert // tile)
            inner = pl.ds(pl.multiple_of((i % (per_expert // tile)) * tile, tile), tile)
            at = pl.ds(pl.multiple_of(i * tile, tile), tile)
            if tensor == 0:
                value = jnp.dot(act_ref[at, :], w_out_ref[expert], preferred_element_type=jnp.float32)
            else:
                value = lax.dot_general(
                    delta_ref[at, :],
                    w_in_ref[expert],
                    (((1,), (1,)), ((), ())),
                    preferred_element_type=jnp.float32,
                )
            sent[tensor, expert, inner, :] = value.astype(jnp.bfloat16)
            return carry

        lax.fori_loop(0, total // tile, body, 0)
        for b in (1, 0):

            def go(j, carry):
                back_copy(tensor, b, j).start()
                return carry

            lax.fori_loop(1, MATES, go, 0)
            ret[tensor, b, mate] = sent[tensor, :, piece(mate, b), :]

    def combine(tensor, b):
        def body(j, carry):
            back_copy(tensor, b, j).wait_recv()
            return carry

        lax.fori_loop(1, MATES, body, 0)
        value = ret[tensor, b].reshape(per_expert, width)
        over_slots = (((0,), (0,)), ((), ()))
        if tensor == 1:
            return lax.dot_general(hot[b], value, over_slots, preferred_element_type=jnp.float32)
        level = gate[b]
        value = value.astype(jnp.float32) * jnp.concatenate([level] * (width // 128), axis=1)
        high = value.astype(jnp.bfloat16)
        low = (value - high.astype(jnp.float32)).astype(jnp.bfloat16)
        return lax.dot_general(
            hot[b], high, over_slots, preferred_element_type=jnp.float32
        ) + lax.dot_general(hot[b], low, over_slots, preferred_element_type=jnp.float32)

    def half_copy(tensor):
        return across_copy(3 + tensor, half_sent.at[tensor], half_came.at[tensor])

    def combine_other(tensor):
        half_sent[tensor] = combine(tensor, 1).astype(jnp.bfloat16)
        half_copy(tensor).start()

    def combine_own(tensor, out_ref):
        mine = combine(tensor, 0)
        half_copy(tensor).wait_recv()
        out_ref[...] = (mine + half_came[tensor].astype(jnp.float32)).astype(jnp.bfloat16)

    def weight_gradient_out(expert):
        tile = 256
        rows = pl.ds(expert * per_expert, per_expert)

        def body(i, carry):
            columns = pl.ds(pl.multiple_of(i * tile, tile), tile)
            gw_out_ref[expert, columns, :] = lax.dot_general(
                act_ref[rows, columns],
                grads_ref[expert],
                (((0,), (0,)), ((), ())),
                preferred_element_type=jnp.float32,
            )
            return carry

        lax.fori_loop(0, units // tile, body, 0)

    def weight_gradient_in(expert):
        tile = 256
        rows = pl.ds(expert * per_expert, per_expert)

        def body(i, carry):
            columns = pl.ds(pl.multiple_of(i * tile, tile), tile)
            gw_in_ref[expert, :, columns] = lax.dot_general(
                rows_ref[expert],
                delta_ref[rows, columns],
                (((0,), (0,)), ((), ())),
                preferred_element_type=jnp.float32,
            )
            return carry

        lax.fori_loop(0, units // tile, body, 0)

    pl.semaphore_wait(barrier, len(partners) + MATES)
    info_copy = across_copy(0, info_ref, info_other)
    grad_copy = across_copy(1, grad_out_ref, grad_out_other)
    token_copy = across_copy(2, tokens_ref, tokens_other)
    info_copy.start()
    grad_copy.start()
    token_copy.start()
    build_map(0)
    dispatch(1, 0)
    dispatch(0, 0)
    info_copy.wait_recv()
    build_map(1)
    grad_copy.wait_recv()
    dispatch(1, 1)
    for b in (0, 1):
        arrived(1, b)

    multiplied = set()
    for number in ORDER:
        wait, tensor, g, gather, k = decoded(number)
        if not wait and not gather and k == 0:
            if tensor == 0 and not multiplied & {(0, n) for n in range(count)}:
                token_copy.wait_recv()
                dispatch(0, 1)
                for b in (0, 1):
                    arrived(0, b)
            multiplied.add((tensor, g))
            partial_products(tensor, g)
        copy = (ag_copy if gather else rs_copy)(tensor, g, k)
        if not wait:
            copy.start()
            continue
        copy.wait_recv()
        if gather:
            multiplied.add((tensor, g, k))
            if k == 0 and tensor == 0 and all((0, n, 0) in multiplied for n in range(count)):
                for b in (0, 1):

                    def left(j, carry):
                        for t in (0, 1):
                            route_copy(t, b, j).wait_send()
                        return carry

                    lax.fori_loop(1, MATES, left, 0)
                results(0)
        elif k < STEPS - 1:
            add(tensor, g, k)
        else:
            multiplied.add((tensor, g, "summed"))
            if all((t, g, "summed") in multiplied for t in (0, 1)):
                activate(g)

    results(1)
    for expert in range(EXP_DEV):
        weight_gradient_out(expert)
    combine_other(0)
    combine_other(1)
    for expert in range(EXP_DEV):
        weight_gradient_in(expert)
    combine_own(0, mixed_ref)
    combine_own(1, grad_tokens_ref)

    for copy in (info_copy, grad_copy, token_copy, half_copy(0), half_copy(1)):
        copy.wait_send()
    for t in (0, 1):
        for b in (0, 1):

            def done(j, carry):
                back_copy(t, b, j).wait_send()
                return carry

            lax.fori_loop(1, MATES, done, 0)
        for g in range(count):
            for k in range(STEPS):
                rs_copy(t, g, k).wait_send()
                ag_copy(t, g, k).wait_send()


def layer(tokens, grad_out, info, w_in, w_out):
    tok_rows, width = tokens.shape
    units = w_in.shape[2]
    per_expert = 2 * tok_rows
    total = EXP_DEV * per_expert
    cap = per_expert // (2 * MATES)
    half, full = jnp.bfloat16, jnp.float32
    vmem, dma = pltpu.VMEM, pltpu.SemaphoreType.DMA
    count = len(GROUPS)
    return pl.pallas_call(
        layer_kernel,
        out_shape=(
            jax.ShapeDtypeStruct(tokens.shape, half),
            jax.ShapeDtypeStruct(tokens.shape, half),
            jax.ShapeDtypeStruct(w_in.shape, full),
            jax.ShapeDtypeStruct(w_out.shape, full),
        ),
        in_specs=[pl.BlockSpec(memory_space=vmem)] * 5,
        out_specs=[pl.BlockSpec(memory_space=vmem)] * 4,
        scratch_shapes=[vmem((total, c), half) for c, _ in GROUPS] * 2
        + [vmem((total - total // 16, c), half) for c, _ in GROUPS] * 2
        + [
            vmem((total, units), half),
            vmem((total, units), half),
            vmem((EXP_DEV, per_expert, width), half),
            vmem((EXP_DEV, per_expert, width), half),
            vmem(info.shape, full),
            vmem(tokens.shape, half),
            vmem(tokens.shape, half),
            vmem((2, per_expert, tok_rows), half),
            vmem((2, per_expert, 128), full),
            vmem((2, EXP_DEV, per_expert, width), half),
            vmem((2, 2, MATES, EXP_DEV, cap, width), half),
            vmem((2, tok_rows, width), half),
            vmem((2, tok_rows, width), half),
        ]
        + [dma((2, count, STEPS))] * 4
        + [dma((2, 2, MATES))] * 4
        + [dma((5,))] * 2,
        compiler_params=pltpu.CompilerParams(
            collective_id=0, has_side_effects=True, vmem_limit_bytes=61 * 2**20
        ),
        name="layer",
    )(tokens, grad_out, info, w_in, w_out)


def body(tokens, expert_ids, gate_values, w_in, w_out, grad_out):
    tok_rows = tokens.shape[0]
    num_experts = EXP_DEV * lax.axis_size("expert")
    capacity = 2 * tok_rows * TOP // num_experts
    slots = slot_index(expert_ids, num_experts, capacity).reshape(tok_rows, TOP)
    info = jnp.concatenate(
        [slots.T.astype(jnp.float32), gate_values.T, jnp.zeros((8 - 2 * TOP, tok_rows), jnp.float32)]
    )
    return layer(tokens, grad_out, info, w_in, w_out)


def solution(mesh):
    return jax.shard_map(
        body,
        mesh=mesh,
        in_specs=(
            P("expert", "dp"),
            P("expert", None),
            P("expert", None),
            P("expert", "dp", None),
            P("expert", None, "dp"),
            P("expert", "dp"),
        ),
        out_specs=(
            P("expert", "dp"),
            P("expert", "dp"),
            P("expert", "dp", None),
            P("expert", None, "dp"),
        ),
        check_vma=False,
    )
```

time: 424 us -> 281 us (0.66)
  starting transfers between devices: 45 us -> 0 us
  waiting for transfers between devices: 38.1 us -> 0 us
  matrix products: 23.7 us -> 0.54 us
  Pallas kernels: 277 us -> 262 us
  local copies, waits for them, and re-layouts: 24.7 us -> 10.3 us
  other arithmetic: 12.8 us -> 2.07 us
    all_to_all x4 -> x0, starting transfers between devices: 45 us -> none  [exchange(): lax.all_to_all(slot_rows, 'expert', split_axis=0, concat_axis=0, tiled=True)]
    all_to_all x4 -> x0, waiting for transfers between devices: 38.1 us -> none  [exchange(): lax.all_to_all(slot_rows, 'expert', split_axis=0, concat_axis=0, tiled=True)]
    dot_general x4 -> x0, matrix products: 23.1 us -> none  [the longest x1 7.26 us: body(): grad_w_out = product('lrh,lrd->lhd', act, grads)]
    pallas_call x1, Pallas kernels: 277 us -> 262 us  [layer(): pl.pallas_call(layer_kernel, out_shape=(jax.ShapeDtypeStruct(tokens.shape...]
    gather x2 -> x0, local copies, waits for them, and re-layouts: 8.87 us -> none  [send_back(): return back[slots].reshape(tok_rows, TOP, width).astype(jnp.float32)]
    unnamed x6 -> x7, local copies, waits for them, and re-layouts: 1.66 us -> 9.74 us
    scatter x1 -> x0, other arithmetic: 6.48 us -> none  [dispatch(): sent = jnp.zeros((total, width), jnp.bfloat16).at[slots].set(rows)]
    scatter x1 -> x0, local copies, waits for them, and re-layouts: 6.01 us -> none  [dispatch(): sent = jnp.zeros((total, width), jnp.bfloat16).at[slots].set(rows)]
  transfers between devices with their start and end apart: 4 -> 0, of which waited for: 3 -> 0; matrix products, arithmetic and copies ran while one was open for 9% -> 0% of each run, Pallas kernels for 0% -> 0%
where the time goes in v3:
time: 281 us; the launch traced here: 276 us
  Pallas kernels  262 us (93%)
  local copies, waits for them, and re-layouts  10.3 us (4%)
    pallas_call x1, Pallas kernels, layer(): pl.pallas_call(layer_kernel, out_shape=(jax.ShapeDtypeStruct(tokens.shape...  262 us
    unnamed x7, local copies, waits for them, and re-layouts  9.74 us

profile of v3, /device:TPU:8, one launch (start us, length us, event | category | flops | bytes accessed | tf_op | source)
XLA Modules:
  0.0 276.1 jit_solution(12606723098958860784)
XLA Ops:
  0.6 0.1 pad.2.clone
  0.7 0.8 copy.10
  1.5 0.2 eq.15
  1.7 0.5 fusion.2
  2.3 0.2 convert_element_type.16
  2.5 0.1 copy.11
  2.6 0.7 convert_bitcast_fusion
  3.3 1.4 maximum_maximum_fusion.info_ref
  4.7 262.5 %layer.1 = (bf16[512,256]{1,0:T(8,128)(2,1)}, bf16[512,256]{1,0:T(8,128)(2,1)}, f32[2,256,1536]{2,1,0:T(8,128)}, f32[2,1536,256]{2,1,0:T(8,128)}) custom-call(bf16[512,256]{1,0:T(8,128)(2,1)} %tokens_ref.1, bf16[512,256]{1,0:T(8,128)(2,1)} %grad_out_ref.1, f32[8,512]{1,0:T(8,128)} %maximum_maximum_fusion.info_ref, bf16[2,256,1536]{2,1,0:T(8,128)(2,1)} %w_in_ref.1, ...), custom_call_target="tpu_custom_call" | custom-call | tf_op jit(solution)/shard_map/layer/pallas_call | solution.py:473
  267.1 1.7 copy.16
  268.8 1.7 copy.17
  270.5 0.0 copy-start
  270.5 3.9 %copy.18 = f32[2,256,1536]{2,1,0:T(8,128)} copy(f32[2,256,1536]{2,1,0:T(8,128)} %get-tuple-element.10) | data formatting | bytes 6291456
  274.4 0.0 copy-done
  274.4 1.7 copy.19
  (2 shorter events, 0.0 us)
Async XLA Ops:
  270.5 3.9 %copy-start = (f32[2,1536,256]{2,1,0:T(8,128)S(1)}, f32[2,1536,256]{2,1,0:T(8,128)}, u32[]{:S(2)}) copy-start(f32[2,1536,256]{2,1,0:T(8,128)} %get-tuple-element.11) | copy-start | bytes 9437188

commit v4 on v3

v4 whole, which is shorter than its diff:
```python
import functools

import jax
import jax.numpy as jnp
from jax import lax
from jax.experimental import pallas as pl
from jax.experimental.pallas import tpu as pltpu
from jax.sharding import PartitionSpec as P

TOP = 2
EXP_DEV = 2
MESH = pl.DeviceIdType.MESH
STEPS = 4
MATES = 8
GROUPS = (
    (0, 256, (1, 0, 2, 3)),
    (0, 256, (0, 1, 2, 3)),
    (0, 256, (2, 0, 1, 3)),
    (0, 256, (2, 1, 0, 3)),
    (0, 256, (0, 1, 2, 3)),
    (0, 256, (1, 0, 2, 3)),
    (1, 256, (0, 1, 2, 3)),
    (1, 256, (1, 0, 2, 3)),
    (1, 256, (2, 1, 0, 3)),
    (1, 256, (2, 0, 1, 3)),
    (1, 256, (0, 1, 2, 3)),
    (1, 256, (1, 0, 2, 3)),
)
FIRST = tuple(sum(q[1] for q in GROUPS[:g] if q[0] == GROUPS[g][0]) for g in range(len(GROUPS)))
ORDER = (
    128, 136, 112, 120, 96, 104, 16, -1, 24, 32, 40, 0, 8, -2, 320, 176, 328, 184, 304, 64, 288, 129, 312, 72,
    296, 48, 208, 160, 216, 168, 224, 17, 232, 25, 192, 33, 200, 41, 321, 56, 368, 1, 376, 177, 209, 185, 217,
    18, 225, 9, 233, 26, 256, 34, 240, 137, 264, 42, 210, 19, 65, 193, 73, 218, 27, 80, 352, 2, 360, 130, 377,
    169, 369, 49, 211, 23, 226, 35, 178, 219, 31, 201, 161, 248, 88, 234, 43, 186, 329, 57, 215, 257, 121,
    227, 39, 194, 3, 10, 223, 322, 131, 138, 235, 47, 265, 66, 370, 241, 74, 50, 361, 113, 378, 231, 179, 38,
    353, 170, 195, 187, 323, 7, 249, 162, 239, 135, 371, 258, 67, 144, 272, 97, 266, 81, 202, 58, 313, 152,
    330, 46, 379, 75, 305, 122, 362, 114, 242, 280, 105, 199, 51, 6, 354, 89, 327, 163, 230, 134, 259, 171,
    267, 71, 250, 243, 59, 273, 82, 37, 238, 314, 45, 289, 98, 30, 306, 22, 355, 167, 363, 175, 263, 79, 251,
    11, 198, 326, 297, 133, 106, 281, 70, 90, 359, 139, 336, 166, 222, 5, 214, 145, 274, 367, 83, 344, 174,
    271, 55, 290, 203, 63, 237, 153, 229, 78, 331, 115, 262, 36, 358, 21, 275, 87, 298, 282, 247, 54, 91, 325,
    165, 197, 132, 255, 62, 123, 366, 69, 337, 44, 146, 270, 4, 307, 183, 279, 86, 99, 283, 95, 315, 191, 246,
    345, 173, 154, 375, 107, 213, 77, 291, 15, 357, 53, 254, 164, 287, 103, 261, 29, 383, 143, 299, 111, 338,
    68, 278, 94, 207, 147, 295, 119, 335, 127, 346, 182, 303, 155, 228, 61, 365, 339, 151, 269, 324, 311, 245,
    85, 52, 319, 126, 221, 118, 253, 347, 159, 236, 60, 196, 343, 286, 150, 93, 318, 125, 351, 374, 158, 310,
    181, 117, 277, 84, 342, 149, 172, 350, 76, 285, 157, 317, 92, 244, 356, 190, 373, 180, 260, 14, 309, 341,
    148, 252, 349, 156, 382, 189, 102, 206, 13, 110, 276, 284, 294, 101, 142, 364, 20, 302, 109, 28, 268, 116,
    205, 334, 124, 381, 188, 12, 348, 372, 141, 301, 293, 100, 108, -3, 340, 380, 333, 140, 292, 204, -4, 300,
    212, 220, 308, 332, -5, 316, -9, -6, -10, -7, -11, -8, -12,
)


def decoded(number):
    rest, k = divmod(number, STEPS)
    rest, gather = divmod(rest, 2)
    rest, g = divmod(rest, len(GROUPS))
    wait, tensor = divmod(rest, 2)
    return wait, tensor, g, gather, k


def gelu_parts(pre):
    scale, cubic = 0.7978845608028654, 0.044715
    square = pre * pre
    tanh = jnp.tanh(scale * (pre + cubic * square * pre))
    half = 0.5 * (1.0 + tanh)
    slope = half + 0.5 * pre * (1.0 - tanh * tanh) * (scale * (1.0 + 3.0 * cubic * square))
    return pre * half, slope


def partners_of(dp):
    x, z = dp // 4, dp % 4
    x0, x1, z0, z1 = x % 2, x // 2, z % 2, z // 2

    def at(a1, a0, c1, c0):
        return (a1 * 2 + a0) * 4 + c1 * 2 + c0

    return (
        (at(x1, 1 - x0, z1, z0), (x0 + x1) % 2),
        (at(1 - x1, 1 - x0, z1, z0), x1),
        (at(x1, x0, z1, 1 - z0), z0),
        (at(x1, x0, 1 - z1, z0), z1),
    )


def layer_kernel(
    tokens_ref, grad_out_ref, ids_ref, gates_ref, w_in_ref, w_out_ref, mixed_ref, grad_tokens_ref, gw_in_out, gw_out_out, *scratch
):
    count = len(GROUPS)
    work = (scratch[0:count], scratch[count : 2 * count])
    recv = (scratch[2 * count : 3 * count], scratch[3 * count : 4 * count])
    (
        act_ref, delta_ref, rows_ref, grads_ref, info_own, info_other, tokens_other, grad_out_other, hot, gate,
        sent, ret, half_sent, half_came, gw_in_ref, gw_out_ref, gw_sem,
        rs_send, rs_recv, ag_send, ag_recv, y_send, y_recv, b_send, b_recv, h_send, h_recv,
    ) = scratch[4 * count :]
    dp, ex = lax.axis_index("dp"), lax.axis_index("expert")
    zh, mate = ex // MATES, ex % MATES
    across = (1 - zh) * MATES + mate
    partners = partners_of(dp)
    tok_rows, width = tokens_ref.shape
    half = rows_ref.shape[2]
    per_expert = 2 * half
    total = EXP_DEV * half
    units = act_ref.shape[2]
    cap = half // MATES
    num_experts = EXP_DEV * 2 * MATES
    outs = (act_ref, delta_ref)
    routed = (rows_ref, grads_ref)

    barrier = pltpu.get_barrier_semaphore()
    for other, _ in partners:
        pl.semaphore_signal(barrier, inc=1, device_id=(other, ex), device_id_type=MESH)
    pl.semaphore_signal(barrier, inc=1, device_id=(dp, across), device_id_type=MESH)
    for j in range(1, MATES):
        near = zh * MATES + (mate + j) % MATES
        pl.semaphore_signal(barrier, inc=1, device_id=(dp, near), device_id_type=MESH)

    def build_map(b):
        source = info_own if b == 0 else info_other
        tile = 128
        expert = lax.broadcasted_iota(jnp.int32, (num_experts, tok_rows), 0).astype(jnp.float32)
        named = [(source[k : k + 1, :] == expert).astype(jnp.float32) for k in range(TOP)]
        earlier = lax.broadcasted_iota(jnp.int32, (tok_rows, tok_rows), 0) < lax.broadcasted_iota(
            jnp.int32, (tok_rows, tok_rows), 1
        )
        before = jnp.dot(
            (named[0] + named[1]).astype(jnp.bfloat16),
            earlier.astype(jnp.float32).astype(jnp.bfloat16),
            preferred_element_type=jnp.float32,
        )
        slots = [
            source[k : k + 1, :] * cap + jnp.sum(named[k] * before, axis=0, keepdims=True) for k in range(TOP)
        ]

        def body(i, carry):
            at = pl.ds(pl.multiple_of(i * tile, tile), tile)
            slot = (
                lax.broadcasted_iota(jnp.int32, (tile, tok_rows), 0) + (zh * per_expert + i * tile)
            ).astype(jnp.float32)
            first, second = slots[0] == slot, slots[1] == slot
            hot[b, at, :] = jnp.where(first, 1.0, jnp.where(second, 1.0, 0.0)).astype(jnp.bfloat16)
            weight = jnp.where(first, source[2:3, :], jnp.where(second, source[3:4, :], 0.0))
            gate[b, at, :] = jnp.broadcast_to(jnp.sum(weight, axis=1, keepdims=True), (tile, 128))
            return carry

        lax.fori_loop(0, per_expert // tile, body, 0)

    def piece(owner):
        return pl.ds(pl.multiple_of(owner * cap, cap), cap)

    def route_copy(tensor, b, j):
        to = (mate + j) % MATES
        return pltpu.make_async_remote_copy(
            src_ref=sent.at[tensor, b, :, piece(to), :],
            dst_ref=routed[tensor].at[b, :, piece(mate), :],
            send_sem=y_send.at[tensor, b, j],
            recv_sem=y_recv.at[tensor, b, j],
            device_id=(dp, zh * MATES + to),
            device_id_type=MESH,
        )

    def route_wait(tensor, b, j):
        return route_copy(tensor, b, j).wait_recv()

    def dispatch(tensor, b):
        block = ((tokens_ref, grad_out_ref), (tokens_other, grad_out_other))[b][tensor]
        near = 4

        def body(i, carry):
            at = pl.ds(pl.multiple_of(i * near * 2 * cap, near * 2 * cap), near * 2 * cap)
            picked = jnp.dot(hot[b, at, :], block[...], preferred_element_type=jnp.float32)
            if tensor == 1:
                level = gate[b, at, :]
                picked = picked * jnp.concatenate([level] * (width // 128), axis=1)
            picked = picked.astype(jnp.bfloat16)
            for n in range(near):
                for e in range(EXP_DEV):
                    start = (n * EXP_DEV + e) * cap
                    sent[tensor, b, e, piece(i * near + n), :] = picked[start : start + cap, :]
            return carry

        lax.fori_loop(0, MATES // near, body, 0)

        def go(j, carry):
            route_copy(tensor, b, j).start()
            return carry

        lax.fori_loop(1, MATES, go, 0)
        routed[tensor][b, :, piece(mate), :] = sent[tensor, b, :, piece(mate), :]

    def arrived(tensor, b):
        def body(j, carry):
            route_wait(tensor, b, j)
            return carry

        lax.fori_loop(1, MATES, body, 0)

    def across_copy(n, source, target):
        return pltpu.make_async_remote_copy(
            src_ref=source,
            dst_ref=target,
            send_sem=h_send.at[n],
            recv_sem=h_recv.at[n],
            device_id=(dp, across),
            device_id_type=MESH,
        )

    def partial_products(tensor, g):
        b, columns, _ = GROUPS[g]
        first = FIRST[g]

        def body(expert, carry):
            if tensor == 0:
                value = jnp.dot(
                    rows_ref[b, expert],
                    w_in_ref[expert, :, first : first + columns],
                    preferred_element_type=jnp.float32,
                )
            else:
                value = lax.dot_general(
                    grads_ref[b, expert],
                    w_out_ref[expert, first : first + columns, :],
                    (((1,), (1,)), ((), ())),
                    preferred_element_type=jnp.float32,
                )
            work[tensor][g][pl.ds(pl.multiple_of(expert * half, half), half), :] = value.astype(jnp.bfloat16)
            return carry

        lax.fori_loop(0, EXP_DEV, body, 0)

    offsets = [[0] for _ in GROUPS]
    for g, (_, _, order) in enumerate(GROUPS):
        for k in range(STEPS):
            offsets[g].append(offsets[g][k] + partners[order[k]][1] * (total >> (k + 1)))

    def rs_copy(tensor, g, k):
        other, bit = partners[GROUPS[g][2][k]]
        size = total >> (k + 1)
        start = pl.multiple_of(offsets[g][k] + (1 - bit) * size, cap)
        return pltpu.make_async_remote_copy(
            src_ref=work[tensor][g].at[pl.ds(start, size), :],
            dst_ref=recv[tensor][g].at[pl.ds(total - 2 * size, size), :],
            send_sem=rs_send.at[tensor, g, k],
            recv_sem=rs_recv.at[tensor, g, k],
            device_id=(other, ex),
            device_id_type=MESH,
        )

    def ag_copy(tensor, g, k):
        other, _ = partners[GROUPS[g][2][k]]
        size = total >> (k + 1)
        held = outs[tensor].at[
            GROUPS[g][0],
            pl.ds(pl.multiple_of(offsets[g][k + 1], cap), size),
            pl.ds(FIRST[g], GROUPS[g][1]),
        ]
        return pltpu.make_async_remote_copy(
            src_ref=held,
            dst_ref=held,
            send_sem=ag_send.at[tensor, g, k],
            recv_sem=ag_recv.at[tensor, g, k],
            device_id=(other, ex),
            device_id_type=MESH,
        )

    def add(tensor, g, k):
        size = total >> (k + 1)
        tile = cap

        def body(i, carry):
            at = pl.ds(pl.multiple_of(offsets[g][k + 1] + i * tile, tile), tile)
            came = pl.ds(pl.multiple_of(total - 2 * size + i * tile, tile), tile)
            mine = work[tensor][g][at, :].astype(jnp.float32)
            work[tensor][g][at, :] = (
                mine + recv[tensor][g][came, :].astype(jnp.float32)
            ).astype(jnp.bfloat16)
            return carry

        lax.fori_loop(0, size // tile, body, 0)

    def activate(g, what):
        b, columns, _ = GROUPS[g]
        size = total >> STEPS
        tile = 32

        def body(i, carry):
            at = pl.ds(pl.multiple_of(offsets[g][STEPS] + i * tile, tile), tile)
            came = pl.ds(pl.multiple_of(total - 2 * size + i * tile, tile), tile)
            for c in range(0, columns, 128):
                part = slice(c, c + 128)
                there = slice(FIRST[g] + c, FIRST[g] + c + 128)
                pre = work[0][g][at, part].astype(jnp.float32) + recv[0][g][came, part].astype(jnp.float32)
                value, slope = gelu_parts(pre)
                if 0 in what:
                    act_ref[b, at, there] = value.astype(jnp.bfloat16)
                if 1 in what:
                    rise = work[1][g][at, part].astype(jnp.float32) + recv[1][g][came, part].astype(jnp.float32)
                    delta_ref[b, at, there] = (rise * slope).astype(jnp.bfloat16)
            return carry

        lax.fori_loop(0, size // tile, body, 0)

    def back_copy(tensor, b, j):
        to = (mate + j) % MATES
        return pltpu.make_async_remote_copy(
            src_ref=sent.at[tensor, b, :, piece(to), :],
            dst_ref=ret.at[tensor, b, mate],
            send_sem=b_send.at[tensor, b, j],
            recv_sem=b_recv.at[tensor, b, j],
            device_id=(dp, zh * MATES + to),
            device_id_type=MESH,
        )

    def results(tensor, b):
        def left(j, carry):
            route_copy(tensor, b, j).wait_send()
            return carry

        lax.fori_loop(1, MATES, left, 0)

        def body(expert, carry):
            at = pl.ds(pl.multiple_of(expert * half, half), half)
            if tensor == 0:
                value = jnp.dot(act_ref[b, at, :], w_out_ref[expert], preferred_element_type=jnp.float32)
            else:
                value = lax.dot_general(
                    delta_ref[b, at, :],
                    w_in_ref[expert],
                    (((1,), (1,)), ((), ())),
                    preferred_element_type=jnp.float32,
                )
            sent[tensor, b, expert] = value.astype(jnp.bfloat16)
            return carry

        lax.fori_loop(0, EXP_DEV, body, 0)

        def go(j, carry):
            back_copy(tensor, b, j).start()
            return carry

        lax.fori_loop(1, MATES, go, 0)
        ret[tensor, b, mate] = sent[tensor, b, :, piece(mate), :]

    def combine(tensor, b):
        def body(j, carry):
            back_copy(tensor, b, j).wait_recv()
            return carry

        lax.fori_loop(1, MATES, body, 0)
        value = ret[tensor, b].reshape(per_expert, width)
        over_slots = (((0,), (0,)), ((), ()))
        if tensor == 1:
            return lax.dot_general(hot[b], value, over_slots, preferred_element_type=jnp.float32)
        level = gate[b]
        value = value.astype(jnp.float32) * jnp.concatenate([level] * (width // 128), axis=1)
        high = value.astype(jnp.bfloat16)
        low = (value - high.astype(jnp.float32)).astype(jnp.bfloat16)
        return lax.dot_general(
            hot[b], high, over_slots, preferred_element_type=jnp.float32
        ) + lax.dot_general(hot[b], low, over_slots, preferred_element_type=jnp.float32)

    def half_copy(tensor):
        return across_copy(3 + tensor, half_sent.at[tensor], half_came.at[tensor])

    def combine_other(tensor):
        half_sent[tensor] = combine(tensor, 1).astype(jnp.bfloat16)
        half_copy(tensor).start()

    def combine_own(tensor, out_ref):
        mine = combine(tensor, 0)
        half_copy(tensor).wait_recv()
        out_ref[...] = (mine + half_came[tensor].astype(jnp.float32)).astype(jnp.bfloat16)

    def weight_gradient(tensor, expert, part):
        tile = 256
        parts = units // tile // 2
        over_rows = (((0,), (0,)), ((), ()))

        def product(left, right):
            return lax.dot_general(left, right, over_rows, preferred_element_type=jnp.float32)

        def body(i, carry):
            columns = pl.ds(pl.multiple_of((part * parts + i) * tile, tile), tile)
            rows = pl.ds(expert * half, half)
            if tensor == 0:
                gw_out_ref[expert, columns, :] = product(act_ref[0, rows, columns], grads_ref[0, expert]) + product(
                    act_ref[1, rows, columns], grads_ref[1, expert]
                )
            else:
                gw_in_ref[expert, :, columns] = product(rows_ref[0, expert], delta_ref[0, rows, columns]) + product(
                    rows_ref[1, expert], delta_ref[1, rows, columns]
                )
            return carry

        lax.fori_loop(0, parts, body, 0)
        weight_copy(tensor, expert, part).start()

    def weight_copy(tensor, expert, part):
        columns = pl.ds(part * (units // 2), units // 2)
        source, target = ((gw_out_ref, gw_out_out), (gw_in_ref, gw_in_out))[tensor]
        place = (expert, columns, slice(None)) if tensor == 0 else (expert, slice(None), columns)
        return pltpu.make_async_copy(source.at[place], target.at[place], gw_sem.at[tensor, expert, part])

    pl.semaphore_wait(barrier, len(partners) + MATES)
    info_copy = across_copy(0, info_own, info_other)
    grad_copy = across_copy(1, grad_out_ref, grad_out_other)
    token_copy = across_copy(2, tokens_ref, tokens_other)
    info_own[0:TOP, :] = ids_ref[...].astype(jnp.float32)
    info_own[TOP : 2 * TOP, :] = gates_ref[...]
    info_own[2 * TOP :, :] = jnp.zeros((8 - 2 * TOP, tok_rows), jnp.float32)
    info_copy.start()
    grad_copy.start()
    token_copy.start()
    build_map(0)
    dispatch(1, 0)
    dispatch(0, 0)

    seen = set()

    def other_grads():
        info_copy.wait_recv()
        build_map(1)
        grad_copy.wait_recv()
        dispatch(1, 1)

    def other_tokens():
        token_copy.wait_recv()
        dispatch(0, 1)

    extra = {
        -1: other_grads,
        -2: other_tokens,
        -3: functools.partial(combine_other, 0),
        -4: functools.partial(combine_other, 1),
    }
    for n in range(4):
        extra[-5 - n] = functools.partial(weight_gradient, 0, n // 2, n % 2)
        extra[-9 - n] = functools.partial(weight_gradient, 1, n // 2, n % 2)
    for number in ORDER:
        if number < 0:
            extra[number]()
            continue
        wait, tensor, g, gather, k = decoded(number)
        b = GROUPS[g][0]
        if not wait and not gather and k == 0:
            if (tensor, b) not in seen:
                seen.add((tensor, b))
                arrived(tensor, b)
            partial_products(tensor, g)
        copy = (ag_copy if gather else rs_copy)(tensor, g, k)
        if not wait:
            copy.start()
            continue
        copy.wait_recv()
        seen.add((tensor, g, gather, k))
        if gather:
            if k == 0 and all((tensor, n, 1, 0) in seen for n in range(count) if GROUPS[n][0] == b):
                results(tensor, b)
        elif k < STEPS - 1:
            add(tensor, g, k)
        elif tensor == 0:
            activate(g, (0, 1) if (1, g, 0, k) in seen else (0,))
        elif (0, g, 0, k) in seen:
            activate(g, (1,))
    combine_own(0, mixed_ref)
    combine_own(1, grad_tokens_ref)

    for copy in (info_copy, grad_copy, token_copy, half_copy(0), half_copy(1)):
        copy.wait_send()
    for t in (0, 1):
        for expert in range(EXP_DEV):
            for part in (0, 1):
                weight_copy(t, expert, part).wait()
        for b in (0, 1):

            def done(j, carry):
                back_copy(t, b, j).wait_send()
                return carry

            lax.fori_loop(1, MATES, done, 0)
        for g in range(count):
            for k in range(STEPS):
                rs_copy(t, g, k).wait_send()
                ag_copy(t, g, k).wait_send()


def layer(tokens, grad_out, ids, gates, w_in, w_out):
    tok_rows, width = tokens.shape
    units = w_in.shape[2]
    per_expert = 2 * tok_rows
    total = EXP_DEV * tok_rows
    cap = tok_rows // MATES
    info = (8, tok_rows)
    half, full = jnp.bfloat16, jnp.float32
    vmem, dma = pltpu.VMEM, pltpu.SemaphoreType.DMA
    count = len(GROUPS)
    return pl.pallas_call(
        layer_kernel,
        out_shape=(
            jax.ShapeDtypeStruct(tokens.shape, half),
            jax.ShapeDtypeStruct(tokens.shape, half),
            jax.ShapeDtypeStruct(w_in.shape, full),
            jax.ShapeDtypeStruct(w_out.shape, full),
        ),
        in_specs=[pl.BlockSpec(memory_space=vmem)] * 6,
        out_specs=[pl.BlockSpec(memory_space=vmem)] * 2 + [pl.BlockSpec(memory_space=pl.ANY)] * 2,
        scratch_shapes=[vmem((total, c), half) for _, c, _ in GROUPS] * 2
        + [vmem((total - total // 16, c), half) for _, c, _ in GROUPS] * 2
        + [
            vmem((2, total, units), half),
            vmem((2, total, units), half),
            vmem((2, EXP_DEV, tok_rows, width), half),
            vmem((2, EXP_DEV, tok_rows, width), half),
            vmem(info, full),
            vmem(info, full),
            vmem(tokens.shape, half),
            vmem(tokens.shape, half),
            vmem((2, per_expert, tok_rows), half),
            vmem((2, per_expert, 128), full),
            vmem((2, 2, EXP_DEV, tok_rows, width), half),
            vmem((2, 2, MATES, EXP_DEV, cap, width), half),
            vmem((2, tok_rows, width), half),
            vmem((2, tok_rows, width), half),
            vmem(w_in.shape, full),
            vmem(w_out.shape, full),
            dma((2, EXP_DEV, 2)),
        ]
        + [dma((2, count, STEPS))] * 4
        + [dma((2, 2, MATES))] * 4
        + [dma((5,))] * 2,
        compiler_params=pltpu.CompilerParams(
            collective_id=0, has_side_effects=True, vmem_limit_bytes=61 * 2**20
        ),
        name="layer",
    )(tokens, grad_out, ids, gates, w_in, w_out)


def body(tokens, expert_ids, gate_values, w_in, w_out, grad_out):
    return layer(tokens, grad_out, expert_ids.T, gate_values.T, w_in, w_out)


def solution(mesh):
    return jax.shard_map(
        body,
        mesh=mesh,
        in_specs=(
            P("expert", "dp"),
            P("expert", None),
            P("expert", None),
            P("expert", "dp", None),
            P("expert", None, "dp"),
            P("expert", "dp"),
        ),
        out_specs=(
            P("expert", "dp"),
            P("expert", "dp"),
            P("expert", "dp", None),
            P("expert", None, "dp"),
        ),
        check_vma=False,
    )
```

time: 281 us -> 247 us (0.88); the launches traced: 276 us -> 247 us
  Pallas kernels: 262 us -> 238 us
    pallas_call x1, Pallas kernels: 262 us -> 238 us  [layer(): pl.pallas_call(layer_kernel, out_shape=(jax.ShapeDtypeStruct(tokens.shape...]
    unnamed x7 -> x6, local copies, waits for them, and re-layouts: 9.74 us -> 8.91 us
where the time goes in v4:
time: 247 us
  Pallas kernels  238 us (96%)
  local copies, waits for them, and re-layouts  8.91 us (4%)
    pallas_call x1, Pallas kernels, layer(): pl.pallas_call(layer_kernel, out_shape=(jax.ShapeDtypeStruct(tokens.shape...  238 us
    unnamed x6, local copies, waits for them, and re-layouts  8.91 us

profile of v4, /device:TPU:8, one launch (start us, length us, event | category | flops | bytes accessed | tf_op | source)
XLA Modules:
  0.0 247.2 jit_solution(2433678788310218008)
XLA Ops:
  0.6 237.6 %layer.1 = (bf16[512,256]{1,0:T(8,128)(2,1)}, bf16[512,256]{1,0:T(8,128)(2,1)}, f32[2,256,1536]{2,1,0:T(8,128)}, f32[2,1536,256]{2,1,0:T(8,128)}) custom-call(bf16[512,256]{1,0:T(8,128)(2,1)} %tokens_ref.1, bf16[512,256]{1,0:T(8,128)(2,1)} %grad_out_ref.1, s32[2,512]{1,0:T(2,128)} %bitcast.2, f32[2,512]{1,0:T(2,128)} %bitcast.3, ...), custom_call_target="tpu_custom_call" | custom-call | tf_op jit(solution)/shard_map/layer/pallas_call | solution.py:496
  238.3 1.7 copy.14
  240.0 1.7 copy.15
  241.6 0.0 copy-start
  241.6 3.9 %copy.16 = f32[2,256,1536]{2,1,0:T(8,128)} copy(f32[2,256,1536]{2,1,0:T(8,128)} %get-tuple-element.10) | data formatting | bytes 6291456
  245.5 0.0 copy-done
  245.5 1.7 copy.17
Async XLA Ops:
  241.6 3.9 %copy-start = (f32[2,1536,256]{2,1,0:T(8,128)S(1)}, f32[2,1536,256]{2,1,0:T(8,128)}, u32[]{:S(2)}) copy-start(f32[2,1536,256]{2,1,0:T(8,128)} %get-tuple-element.11) | copy-start | bytes 9437188

commit v5 on v4

--- a/solution.py
+++ b/solution.py
@@ -13,39 +13,39 @@
 STEPS = 4
 MATES = 8
 GROUPS = (
+    (0, 256, (0, 1, 2, 3)),
     (0, 256, (1, 0, 2, 3)),
     (0, 256, (0, 1, 2, 3)),
-    (0, 256, (2, 0, 1, 3)),
-    (0, 256, (2, 1, 0, 3)),
-    (0, 256, (0, 1, 2, 3)),
     (0, 256, (1, 0, 2, 3)),
+    (0, 256, (1, 0, 3, 2)),
+    (0, 256, (0, 1, 3, 2)),
+    (1, 256, (2, 0, 1, 3)),
+    (1, 256, (2, 1, 0, 3)),
     (1, 256, (0, 1, 2, 3)),
     (1, 256, (1, 0, 2, 3)),
-    (1, 256, (2, 1, 0, 3)),
-    (1, 256, (2, 0, 1, 3)),
+    (1, 256, (1, 0, 2, 3)),
     (1, 256, (0, 1, 2, 3)),
-    (1, 256, (1, 0, 2, 3)),
 )
 FIRST = tuple(sum(q[1] for q in GROUPS[:g] if q[0] == GROUPS[g][0]) for g in range(len(GROUPS)))
 ORDER = (
-    128, 136, 112, 120, 96, 104, 16, -1, 24, 32, 40, 0, 8, -2, 320, 176, 328, 184, 304, 64, 288, 129, 312, 72,
-    296, 48, 208, 160, 216, 168, 224, 17, 232, 25, 192, 33, 200, 41, 321, 56, 368, 1, 376, 177, 209, 185, 217,
-    18, 225, 9, 233, 26, 256, 34, 240, 137, 264, 42, 210, 19, 65, 193, 73, 218, 27, 80, 352, 2, 360, 130, 377,
-    169, 369, 49, 211, 23, 226, 35, 178, 219, 31, 201, 161, 248, 88, 234, 43, 186, 329, 57, 215, 257, 121,
-    227, 39, 194, 3, 10, 223, 322, 131, 138, 235, 47, 265, 66, 370, 241, 74, 50, 361, 113, 378, 231, 179, 38,
-    353, 170, 195, 187, 323, 7, 249, 162, 239, 135, 371, 258, 67, 144, 272, 97, 266, 81, 202, 58, 313, 152,
-    330, 46, 379, 75, 305, 122, 362, 114, 242, 280, 105, 199, 51, 6, 354, 89, 327, 163, 230, 134, 259, 171,
-    267, 71, 250, 243, 59, 273, 82, 37, 238, 314, 45, 289, 98, 30, 306, 22, 355, 167, 363, 175, 263, 79, 251,
-    11, 198, 326, 297, 133, 106, 281, 70, 90, 359, 139, 336, 166, 222, 5, 214, 145, 274, 367, 83, 344, 174,
-    271, 55, 290, 203, 63, 237, 153, 229, 78, 331, 115, 262, 36, 358, 21, 275, 87, 298, 282, 247, 54, 91, 325,
-    165, 197, 132, 255, 62, 123, 366, 69, 337, 44, 146, 270, 4, 307, 183, 279, 86, 99, 283, 95, 315, 191, 246,
-    345, 173, 154, 375, 107, 213, 77, 291, 15, 357, 53, 254, 164, 287, 103, 261, 29, 383, 143, 299, 111, 338,
-    68, 278, 94, 207, 147, 295, 119, 335, 127, 346, 182, 303, 155, 228, 61, 365, 339, 151, 269, 324, 311, 245,
-    85, 52, 319, 126, 221, 118, 253, 347, 159, 236, 60, 196, 343, 286, 150, 93, 318, 125, 351, 374, 158, 310,
-    181, 117, 277, 84, 342, 149, 172, 350, 76, 285, 157, 317, 92, 244, 356, 190, 373, 180, 260, 14, 309, 341,
-    148, 252, 349, 156, 382, 189, 102, 206, 13, 110, 276, 284, 294, 101, 142, 364, 20, 302, 109, 28, 268, 116,
-    205, 334, 124, 381, 188, 12, 348, 372, 141, 301, 293, 100, 108, -3, 340, 380, 333, 140, 292, 204, -4, 300,
-    212, 220, 308, 332, -5, 316, -9, -6, -10, -7, -11, -8, -12,
+    96, 104, 112, 120, 128, 136, -1, 288, 40, 296, 97, 304, 105, 328, 0, 312, 113, 320, 32, 144, 152, 289, 98,
+    137, 297, 121, 305, 8, -2, 232, 129, 290, 99, 106, 329, 41, 138, 192, 184, 291, 224, 1, 313, 33, 330, 321,
+    130, 64, 298, 107, 114, 233, 42, 72, 336, 122, 344, 139, 200, 80, 193, 176, 306, 2, 299, 115, 322, 225,
+    34, 9, 331, 131, 234, 376, 88, 314, 123, 43, 307, 194, 3, 48, 323, 56, 226, 235, 35, 256, 16, 315, 195, 7,
+    103, 201, 145, 264, 65, 227, 10, 272, 185, 368, 24, 199, 295, 280, 73, 257, 89, 202, 6, 11, 337, 81, 240,
+    66, 377, 146, 203, 15, 111, 248, 186, 208, 177, 198, 39, 265, 49, 258, 67, 74, 273, 160, 281, 5, 338, 17,
+    216, 57, 207, 147, 303, 259, 71, 231, 14, 38, 378, 82, 266, 90, 339, 75, 369, 25, 197, 153, 241, 4, 263,
+    187, 209, 50, 249, 168, 230, 267, 79, 206, 70, 379, 274, 83, 178, 345, 282, 91, 18, 352, 13, 161, 242,
+    217, 37, 271, 51, 275, 87, 283, 95, 262, 69, 78, 243, 55, 196, 58, 370, 26, 360, 210, 47, 279, 179, 353,
+    287, 19, 205, 12, 154, 247, 54, 191, 229, 169, 270, 86, 261, 36, 250, 68, 371, 59, 239, 94, 346, 77, 211,
+    46, 218, 162, 383, 27, 278, 190, 246, 251, 63, 361, 85, 286, 93, 170, 219, 155, 238, 183, 255, 151, 269,
+    53, 204, 76, 354, 135, 382, 143, 228, 45, 362, 102, 347, 163, 260, 62, 375, 171, 277, 343, 159, 285, 84,
+    92, 327, 182, 335, 110, 245, 294, 52, 254, 355, 167, 363, 175, 351, 158, 134, 237, 61, 44, 374, 302, 284,
+    181, 359, 166, 142, 350, 109, 268, 189, 367, 174, 23, 326, 31, 253, 150, 276, 157, 215, 119, 334, 127,
+    373, 133, 381, 180, 223, 358, 60, 366, 22, 301, 173, 342, 165, 311, 319, 236, 188, 244, 30, 349, 141, 325,
+    149, 214, 156, 222, 118, 365, 29, 357, 172, 372, 132, 252, 126, 333, 21, 310, 341, 164, 148, 380, 140,
+    221, 348, 318, 125, 340, 213, 28, 364, 117, -3, 324, 101, 356, 20, 317, 332, 309, 116, 124, 212, 293, 100,
+    108, 220, -5, -4, -6, -7, 308, -8, 292, 316, 300, -9, -10, -11, -12,
 )
 
 
@@ -82,16 +82,16 @@
 
 
 def layer_kernel(
-    tokens_ref, grad_out_ref, ids_ref, gates_ref, w_in_ref, w_out_ref, mixed_ref, grad_tokens_ref, gw_in_out, gw_out_out, *scratch
+    tokens_ref, grad_out_ref, ids_ref, gates_ref, w_in_arg, w_out_arg, mixed_ref, grad_tokens_ref, gw_in_out, gw_out_out, *scratch
 ):
     count = len(GROUPS)
     work = (scratch[0:count], scratch[count : 2 * count])
     recv = (scratch[2 * count : 3 * count], scratch[3 * count : 4 * count])
     (
-        act_ref, delta_ref, rows_ref, grads_ref, info_own, info_other, tokens_other, grad_out_other, hot, gate,
-        sent, ret, half_sent, half_came, gw_in_ref, gw_out_ref, gw_sem,
+        rows_ref, grads_ref, info_own, info_other, tokens_other, grad_out_other, hot, gate,
+        sent, ret, half_sent, half_came, gw_in_ref, gw_out_ref, gw_sem, w_in_ref, w_out_ref, w_sem,
         rs_send, rs_recv, ag_send, ag_recv, y_send, y_recv, b_send, b_recv, h_send, h_recv,
-    ) = scratch[4 * count :]
+    ) = scratch[6 * count :]
     dp, ex = lax.axis_index("dp"), lax.axis_index("expert")
     zh, mate = ex // MATES, ex % MATES
     across = (1 - zh) * MATES + mate
@@ -100,11 +100,16 @@
     half = rows_ref.shape[2]
     per_expert = 2 * half
     total = EXP_DEV * half
-    units = act_ref.shape[2]
+    units = w_in_ref.shape[2]
     cap = half // MATES
     num_experts = EXP_DEV * 2 * MATES
-    outs = (act_ref, delta_ref)
+    outs = (scratch[4 * count : 5 * count], scratch[5 * count : 6 * count])
     routed = (rows_ref, grads_ref)
+
+    weights_in = pltpu.make_async_copy(w_in_arg, w_in_ref, w_sem.at[0])
+    weights_out = pltpu.make_async_copy(w_out_arg, w_out_ref, w_sem.at[1])
+    weights_out.start()
+    weights_in.start()
 
     barrier = pltpu.get_barrier_semaphore()
     for other, _ in partners:
@@ -248,11 +253,7 @@
     def ag_copy(tensor, g, k):
         other, _ = partners[GROUPS[g][2][k]]
         size = total >> (k + 1)
-        held = outs[tensor].at[
-            GROUPS[g][0],
-            pl.ds(pl.multiple_of(offsets[g][k + 1], cap), size),
-            pl.ds(FIRST[g], GROUPS[g][1]),
-        ]
+        held = outs[tensor][g].at[pl.ds(pl.multiple_of(offsets[g][k + 1], cap), size), :]
         return pltpu.make_async_remote_copy(
             src_ref=held,
             dst_ref=held,
@@ -278,7 +279,7 @@
         lax.fori_loop(0, size // tile, body, 0)
 
     def activate(g, what):
-        b, columns, _ = GROUPS[g]
+        columns = GROUPS[g][1]
         size = total >> STEPS
         tile = 32
 
@@ -287,14 +288,13 @@
             came = pl.ds(pl.multiple_of(total - 2 * size + i * tile, tile), tile)
             for c in range(0, columns, 128):
                 part = slice(c, c + 128)
-                there = slice(FIRST[g] + c, FIRST[g] + c + 128)
                 pre = work[0][g][at, part].astype(jnp.float32) + recv[0][g][came, part].astype(jnp.float32)
                 value, slope = gelu_parts(pre)
                 if 0 in what:
-                    act_ref[b, at, there] = value.astype(jnp.bfloat16)
+                    outs[0][g][at, part] = value.astype(jnp.bfloat16)
                 if 1 in what:
                     rise = work[1][g][at, part].astype(jnp.float32) + recv[1][g][came, part].astype(jnp.float32)
-                    delta_ref[b, at, there] = (rise * slope).astype(jnp.bfloat16)
+                    outs[1][g][at, part] = (rise * slope).astype(jnp.bfloat16)
             return carry
 
         lax.fori_loop(0, size // tile, body, 0)
@@ -319,15 +319,22 @@
 
         def body(expert, carry):
             at = pl.ds(pl.multiple_of(expert * half, half), half)
-            if tensor == 0:
-                value = jnp.dot(act_ref[b, at, :], w_out_ref[expert], preferred_element_type=jnp.float32)
-            else:
-                value = lax.dot_general(
-                    delta_ref[b, at, :],
-                    w_in_ref[expert],
-                    (((1,), (1,)), ((), ())),
-                    preferred_element_type=jnp.float32,
-                )
+            value = 0.0
+            for g in range(count):
+                if GROUPS[g][0] != b:
+                    continue
+                part = slice(FIRST[g], FIRST[g] + GROUPS[g][1])
+                if tensor == 0:
+                    value += jnp.dot(
+                        outs[0][g][at, :], w_out_ref[expert, part, :], preferred_element_type=jnp.float32
+                    )
+                else:
+                    value += lax.dot_general(
+                        outs[1][g][at, :],
+                        w_in_ref[expert, :, part],
+                        (((1,), (1,)), ((), ())),
+                        preferred_element_type=jnp.float32,
+                    )
             sent[tensor, b, expert] = value.astype(jnp.bfloat16)
             return carry
 
@@ -371,27 +378,23 @@
         out_ref[...] = (mine + half_came[tensor].astype(jnp.float32)).astype(jnp.bfloat16)
 
     def weight_gradient(tensor, expert, part):
-        tile = 256
-        parts = units // tile // 2
         over_rows = (((0,), (0,)), ((), ()))
+        pairs = [(n, n + count // 2) for n in range(count // 2)]
+        rows = slice(expert * half, (expert + 1) * half)
 
         def product(left, right):
             return lax.dot_general(left, right, over_rows, preferred_element_type=jnp.float32)
 
-        def body(i, carry):
-            columns = pl.ds(pl.multiple_of((part * parts + i) * tile, tile), tile)
-            rows = pl.ds(expert * half, half)
+        for pair in pairs[part * count // 4 : (part + 1) * count // 4]:
+            columns = slice(FIRST[pair[0]], FIRST[pair[0]] + GROUPS[pair[0]][1])
             if tensor == 0:
-                gw_out_ref[expert, columns, :] = product(act_ref[0, rows, columns], grads_ref[0, expert]) + product(
-                    act_ref[1, rows, columns], grads_ref[1, expert]
+                gw_out_ref[expert, columns, :] = sum(
+                    product(outs[0][g][rows, :], grads_ref[GROUPS[g][0], expert]) for g in pair
                 )
             else:
-                gw_in_ref[expert, :, columns] = product(rows_ref[0, expert], delta_ref[0, rows, columns]) + product(
-                    rows_ref[1, expert], delta_ref[1, rows, columns]
+                gw_in_ref[expert, :, columns] = sum(
+                    product(rows_ref[GROUPS[g][0], expert], outs[1][g][rows, :]) for g in pair
                 )
-            return carry
-
-        lax.fori_loop(0, parts, body, 0)
         weight_copy(tensor, expert, part).start()
 
     def weight_copy(tensor, expert, part):
@@ -409,17 +412,19 @@
     info_own[2 * TOP :, :] = jnp.zeros((8 - 2 * TOP, tok_rows), jnp.float32)
     info_copy.start()
     grad_copy.start()
-    token_copy.start()
     build_map(0)
     dispatch(1, 0)
     dispatch(0, 0)
+    weights_out.wait()
+    weights_in.wait()
 
     seen = set()
 
     def other_grads():
+        grad_copy.wait_recv()
+        token_copy.start()
         info_copy.wait_recv()
         build_map(1)
-        grad_copy.wait_recv()
         dispatch(1, 1)
 
     def other_tokens():
@@ -485,7 +490,6 @@
 
 def layer(tokens, grad_out, ids, gates, w_in, w_out):
     tok_rows, width = tokens.shape
-    units = w_in.shape[2]
     per_expert = 2 * tok_rows
     total = EXP_DEV * tok_rows
     cap = tok_rows // MATES
@@ -501,13 +505,12 @@
             jax.ShapeDtypeStruct(w_in.shape, full),
             jax.ShapeDtypeStruct(w_out.shape, full),
         ),
-        in_specs=[pl.BlockSpec(memory_space=vmem)] * 6,
+        in_specs=[pl.BlockSpec(memory_space=vmem)] * 4 + [pl.BlockSpec(memory_space=pl.ANY)] * 2,
         out_specs=[pl.BlockSpec(memory_space=vmem)] * 2 + [pl.BlockSpec(memory_space=pl.ANY)] * 2,
         scratch_shapes=[vmem((total, c), half) for _, c, _ in GROUPS] * 2
         + [vmem((total - total // 16, c), half) for _, c, _ in GROUPS] * 2
+        + [vmem((total, c), half) for _, c, _ in GROUPS] * 2
         + [
-            vmem((2, total, units), half),
-            vmem((2, total, units), half),
             vmem((2, EXP_DEV, tok_rows, width), half),
             vmem((2, EXP_DEV, tok_rows, width), half),
             vmem(info, full),
@@ -523,6 +526,9 @@
             vmem(w_in.shape, full),
             vmem(w_out.shape, full),
             dma((2, EXP_DEV, 2)),
+            vmem(w_in.shape, half),
+            vmem(w_out.shape, half),
+            dma((2,)),
         ]
         + [dma((2, count, STEPS))] * 4
         + [dma((2, 2, MATES))] * 4
@@ -534,8 +540,33 @@
     )(tokens, grad_out, ids, gates, w_in, w_out)
 
 
+def publish_kernel(*refs):
+    count = len(refs) // 2
+    for source, target in zip(refs[:count], refs[count:]):
+        target[...] = source[...]
+
+
+def publish(*arrays):
+    steps = 8
+
+    def block(a):
+        shape = (*a.shape[:-2], a.shape[-2] // steps, a.shape[-1])
+        if len(shape) == 3:
+            return pl.BlockSpec(shape, lambda i: (0, i, 0))
+        return pl.BlockSpec(shape, lambda i: (i, 0))
+
+    return pl.pallas_call(
+        publish_kernel,
+        grid=(steps,),
+        out_shape=tuple(jax.ShapeDtypeStruct(a.shape, a.dtype) for a in arrays),
+        in_specs=[block(a) for a in arrays],
+        out_specs=[block(a) for a in arrays],
+        name="publish",
+    )(*arrays)
+
+
 def body(tokens, expert_ids, gate_values, w_in, w_out, grad_out):
-    return layer(tokens, grad_out, expert_ids.T, gate_values.T, w_in, w_out)
+    return publish(*layer(tokens, grad_out, expert_ids.T, gate_values.T, w_in, w_out))
 
 
 def solution(mesh):

time: 247 us -> 242 us (0.980); the launches traced: 247 us -> 238 us
  local copies, waits for them, and re-layouts: 8.91 us -> 0 us
    unnamed x6 -> x0, local copies, waits for them, and re-layouts: 8.91 us -> none
    pallas_call x1, Pallas kernels: 238 us -> 229 us  [layer(): pl.pallas_call(layer_kernel, out_shape=(jax.ShapeDtypeStruct(tokens.shape...]
    pallas_call x0 -> x1, Pallas kernels: none -> 8.04 us  [publish(): pl.pallas_call(publish_kernel, grid=(steps,), out_shape=tuple((jax.ShapeD...]
where the time goes in v5:
time: 242 us; the launch traced here: 238 us
  Pallas kernels  237 us (98%)
    pallas_call x1, Pallas kernels, layer(): pl.pallas_call(layer_kernel, out_shape=(jax.ShapeDtypeStruct(tokens.shape...  229 us
    pallas_call x1, Pallas kernels, publish(): pl.pallas_call(publish_kernel, grid=(steps,), out_shape=tuple((jax.ShapeD...  8.04 us

profile of v5, /device:TPU:8, one launch (start us, length us, event | category | flops | bytes accessed | tf_op | source)
XLA Modules:
  0.0 238.1 jit_solution(13429222222217802609)
XLA Ops:
  0.6 229.4 %layer.1 = (bf16[512,256]{1,0:T(8,128)(2,1)}, bf16[512,256]{1,0:T(8,128)(2,1)}, f32[2,256,1536]{2,1,0:T(8,128)}, f32[2,1536,256]{2,1,0:T(8,128)}) custom-call(bf16[512,256]{1,0:T(8,128)(2,1)} %tokens_ref.1, bf16[512,256]{1,0:T(8,128)(2,1)} %grad_out_ref.1, s32[2,512]{1,0:T(2,128)} %bitcast.2, f32[2,512]{1,0:T(2,128)} %bitcast.3, ...), custom_call_target="tpu_custom_call" | custom-call | tf_op jit(solution)/shard_map/layer/pallas_call | solution.py:500
  230.1 8.0 %publish.1 = (bf16[512,256]{1,0:T(8,128)(2,1)}, bf16[512,256]{1,0:T(8,128)(2,1)}, f32[2,256,1536]{2,1,0:T(8,128)}, f32[2,1536,256]{2,1,0:T(8,128)}) custom-call(bf16[512,256]{1,0:T(8,128)(2,1)} %get-tuple-element.8.refs_0_, bf16[512,256]{1,0:T(8,128)(2,1)} %get-tuple-element.9.refs_1_, f32[2,256,1536]{2,1,0:T(8,128)} %get-tuple-element.10.refs_2_, ...), custom_call_target="tpu_custom_call" | custom-call | tf_op jit(solution)/shard_map/publish/pallas_call | solution.py:558
